TPU v7x, 512 devices: a whole 4x4x16 slice. The times are simulated.
512 devices in a mesh: dom: 128 (over z, x, core), rep: 4 (over y).
Axes of the slice: x: 4, y: 4, z: 16, core: 2. Of those that a mesh axis runs over, the one named last changes fastest.
Arguments:
- features: bfloat16 [32768, 256], P('dom'), may hold values from -6 to 6
- positions: float32 [3, 32768], P(None, 'dom'), may hold values from -6 to 6
- radial: bfloat16 [8, 256, 256], replicated, may hold values from -0.03125 to 0.03125
- mixing: bfloat16 [256, 256], replicated, may hold values from -0.375 to 0.375
- readout: float32 [256], replicated, may hold values from -4 to 4
- decay: float32 [8], replicated, may hold values from 0.1 to 1
- send_rows: int32 [4, 16384], P(None, 'dom'), may hold values from 0 to 255
- pair_home: int32 [24576], P(('dom', 'rep')), may hold values from 0 to 1
- pair_other: int32 [24576], P(('dom', 'rep')), may hold values from 0 to 5
- pair_kind: int32 [24576], P(('dom', 'rep')), may hold values from 0 to 7
- pair_image: int32 [3, 24576], P(None, ('dom', 'rep')), may hold values from -1 to 1
Outputs:
- grad_features: bfloat16 [32768, 256], P('dom')
- forces: float32 [3, 32768], P(None, 'dom')
- virials: float32 [6, 32768], P(None, 'dom')
- grad_mixing: float32 [256, 256], P('dom', 'rep')
Inputs may be any that keep to these rules, and one draw needn't show every extreme that they name: `send_rows`: rows may repeat within a round.
All inputs are finite; a program needn't handle non-finite values.
Results may differ from a plain program's by a relative error of at most 0.006.
Values may be sent and summed in bfloat16 or wider, within the bound.
No kernel may reach another device: no remote copies, remote signals or barrier semaphores. Data moves between devices by JAX's collectives and lax.ppermute only.
A program may use at most 128 MiB of HBM per device.

v0:
```python
import jax
import jax.numpy as jnp
from jax import lax
from jax.sharding import PartitionSpec as P

TILE_ATOMS = 128


offsets = (1, -1, 2, -2)
cell_edge = 2.0
component_pairs = ((0, 0), (1, 1), (2, 2), (0, 1), (0, 2), (1, 2))
highest_precision = lax.Precision.HIGHEST


def from_behind(array, axis, by):
    count = lax.axis_size(axis)
    return lax.ppermute(array, axis, [(i, (i + by) % count) for i in range(count)])


def pair_setup(ext_feat, ext_pos, pair_home, pair_other, pair_kind, pair_image, radial, decay):
    channel_count = ext_feat.shape[1]
    tiles_feat = ext_feat.reshape(-1, TILE_ATOMS, channel_count)
    tiles_pos = ext_pos.reshape(3, -1, TILE_ATOMS)
    far_end = (
        jnp.take(tiles_pos, pair_other, axis=1)
        + pair_image[:, :, None].astype(jnp.float32) * cell_edge
    )
    near_end = jnp.take(tiles_pos, pair_home, axis=1)
    separation = far_end[:, :, None, :] - near_end[:, :, :, None]
    kind_table = (pair_kind[:, None] == lax.iota(jnp.int32, decay.shape[0])[None, :]).astype(
        jnp.float32
    )
    rates = jnp.sum(kind_table * decay[None, :], axis=1)
    kernel = jnp.exp(-rates[:, None, None] * jnp.sum(separation * separation, axis=0))
    partner_rows = jnp.take(tiles_feat, pair_other, axis=0)
    chosen = jnp.take(radial, pair_kind, axis=0)
    mapped = jnp.einsum(
        "pbc,pcd->pbd", partner_rows, chosen, preferred_element_type=jnp.float32
    ).astype(jnp.bfloat16)
    return (separation, rates, kernel, mapped, chosen)


def atom_section(message, mixing, readout):
    packed = message.astype(jnp.bfloat16)
    mixed_rows = jnp.dot(packed, mixing, preferred_element_type=jnp.float32)
    sigmoid_rows = jax.nn.sigmoid(mixed_rows)
    slope_rows = (readout * sigmoid_rows * (1.0 + mixed_rows * (1.0 - sigmoid_rows))).astype(
        jnp.bfloat16
    )
    adjoint = lax.dot_general(
        slope_rows, mixing, (((1,), (1,)), ((), ())), preferred_element_type=jnp.float32
    ).astype(jnp.bfloat16)
    return (packed, slope_rows, adjoint)


def on_device(
    features,
    positions,
    radial,
    mixing,
    readout,
    decay,
    send_rows,
    pair_home,
    pair_other,
    pair_kind,
    pair_image,
):
    count_of_atoms, channel_count = features.shape
    home_tiles = count_of_atoms // TILE_ATOMS
    extended_tiles = home_tiles + len(offsets)
    halo_feat = []
    halo_pos = []
    for section_no in range(len(offsets)):
        picked_feat = jnp.take(features, send_rows[section_no], axis=0)
        picked_pos = jnp.take(positions, send_rows[section_no], axis=1)
        halo_feat.append(from_behind(picked_feat, "dom", offsets[section_no]))
        halo_pos.append(from_behind(picked_pos, "dom", offsets[section_no]))
    ext_feat = jnp.concatenate([features] + halo_feat, axis=0)
    ext_pos = jnp.concatenate([positions] + halo_pos, axis=1)
    separation, rates, kernel, mapped, chosen = pair_setup(
        ext_feat, ext_pos, pair_home, pair_other, pair_kind, pair_image, radial, decay
    )
    kernel_low = kernel.astype(jnp.bfloat16)
    message_rows = jnp.einsum(
        "pab,pbd->pad", kernel_low, mapped, preferred_element_type=jnp.float32
    )
    home_lookup_table = (pair_home[None, :] == lax.iota(jnp.int32, home_tiles)[:, None]).astype(
        jnp.float32
    )
    partner_table = (pair_other[None, :] == lax.iota(jnp.int32, extended_tiles)[:, None]).astype(
        jnp.float32
    )
    message_portion = jnp.einsum(
        "so,oxe->sxe", home_lookup_table, message_rows, precision=highest_precision
    ).reshape(count_of_atoms, channel_count)
    message = lax.psum(message_portion, "rep")
    packed, slope_rows, adjoint = atom_section(message, mixing, readout)
    column_share = channel_count // lax.axis_size("rep")
    column_start = lax.axis_index("rep") * column_share
    slope_cols = lax.dynamic_slice_in_dim(slope_rows, column_start, column_share, 1)
    mixing_part = lax.dot_general(
        packed, slope_cols, (((0,), (0,)), ((), ())), preferred_element_type=jnp.float32
    )
    grad_mixing = lax.psum_scatter(mixing_part, "dom", scatter_dimension=0, tiled=True)
    adjoint_tiles = jnp.take(
        adjoint.reshape(home_tiles, TILE_ATOMS, channel_count), pair_home, axis=0
    )
    kernel_grad = jnp.einsum(
        "pad,pbd->pab", adjoint_tiles, mapped, preferred_element_type=jnp.float32
    )
    mapped_grad = jnp.einsum(
        "pab,pad->pbd", kernel_low, adjoint_tiles, preferred_element_type=jnp.float32
    ).astype(jnp.bfloat16)
    feature_grad = jnp.einsum(
        "pbd,pcd->pbc", mapped_grad, chosen, preferred_element_type=jnp.float32
    )
    weight = -2.0 * rates[:, None, None] * kernel * kernel_grad
    home_atom_side = []
    partner_side = []
    for axis_one in range(3):
        pull = weight * separation[axis_one]
        home_atom_side.append(jnp.sum(pull, axis=2))
        partner_side.append(-jnp.sum(pull, axis=1))
    for axis_one, axis_two in component_pairs:
        product = weight * separation[axis_one] * separation[axis_two]
        home_atom_side.append(-0.5 * jnp.sum(product, axis=2))
        partner_side.append(-0.5 * jnp.sum(product, axis=1))
    home_atom_side = jnp.stack(home_atom_side)
    partner_side = jnp.stack(partner_side)
    ext_grad = jnp.einsum(
        "jp,pbc->jbc", partner_table, feature_grad, precision=highest_precision
    ).reshape(extended_tiles * TILE_ATOMS, channel_count)
    extended_side = jnp.einsum(
        "it,ztq->ziq", partner_table, partner_side, precision=highest_precision
    ).reshape(9, extended_tiles * TILE_ATOMS)
    self_side = (
        jnp.einsum(
            "qk,gkv->gqv", home_lookup_table, home_atom_side, precision=highest_precision
        ).reshape(9, count_of_atoms)
        + extended_side[:, :count_of_atoms]
    )
    own_grad = ext_grad[:count_of_atoms]
    atom_iota = lax.iota(jnp.int32, count_of_atoms)
    for section_no in range(len(offsets)):
        lower_row = count_of_atoms + section_no * TILE_ATOMS
        returned = (
            ext_grad[lower_row : lower_row + TILE_ATOMS],
            extended_side[:, lower_row : lower_row + TILE_ATOMS],
        )
        received = from_behind((returned[0], returned[1]), "dom", -offsets[section_no])
        send_onehot = (send_rows[section_no][:, None] == atom_iota[None, :]).astype(jnp.float32)
        own_grad = own_grad + jnp.einsum(
            "ta,tc->ac", send_onehot, received[0], precision=highest_precision
        )
        self_side = self_side + jnp.einsum(
            "ta,ct->ca", send_onehot, received[1], precision=highest_precision
        )
    totals = lax.psum((own_grad, self_side), "rep")
    grad_features = totals[0].astype(jnp.bfloat16)
    forces = totals[1][:3]
    virials = totals[1][3:]
    return (grad_features, forces, virials, grad_mixing)


def solution(mesh):
    in_specs = (
        P("dom", None),
        P(None, "dom"),
        P(),
        P(),
        P(),
        P(),
        P(None, "dom"),
        P(("dom", "rep")),
        P(("dom", "rep")),
        P(("dom", "rep")),
        P(None, ("dom", "rep")),
    )
    out_specs = (P("dom", None), P(None, "dom"), P(None, "dom"), P("dom", "rep"))
    return jax.shard_map(
        on_device, mesh=mesh, in_specs=in_specs, out_specs=out_specs, check_vma=False
    )
```

profile of v0, /device:TPU:1, one launch (start us, length us, event | category | flops | bytes accessed | tf_op | source)
XLA Modules:
  0.0 485.1 jit_solution(6648772068461673757)
XLA Ops:
  7.3 0.8 compare_and_fusion.2
  8.1 1.7 gather_fusion.12
  9.9 14.1 %collective-permute-start.7 = (bf16[128,256]{1,0:T(8,128)(2,1)S(1)}, bf16[128,256]{1,0:T(8,128)(2,1)S(1)}, u32[]{:S(2)}, u32[]{:S(2)}) collective-permute-start(bf16[128,256]{1,0:T(8,128)(2,1)S(1)} %broadcast_select_fusion.9), channel_id=1, source_target_pairs={{0,504},{4,508},{8,0},{12,4},{16,8},{20,12},{24,16},{28,20},{32,24... | collective-permute-start | bytes 196616 | tf_op jit(solution)/shard_map/ppermute | solution.py:17
  24.1 1.7 gather_fusion.11
  25.9 1.9 collective-permute-start.6
  27.8 1.7 gather_fusion.10
  29.6 2.9 collective-permute-start.5
  32.5 1.7 gather_fusion.9
  34.2 2.7 collective-permute-start.4
  36.9 0.8 copy.52
  37.8 0.6 gather_fusion.3
  38.5 1.9 collective-permute-start
  40.6 0.6 gather_fusion.6
  41.2 0.6 gather_fusion.5
  41.8 0.6 gather_fusion.4
  43.0 1.3 dynamic-slice
  45.0 4.9 %gather_fusion.1 = bf16[48,256,256]{2,1,0:T(8,128)(2,1)} fusion(bf16[8,256,256]{2,1,0:T(8,128)(2,1)S(1)} %copy-done, s32[1024]{0:T(1024)S(1)} %get-tuple-element.74), kind=kCustom, calls=%fused_computation.11 | custom fusion | bytes 12583104 | tf_op jit(solution)/shard_map/jit(_take)/gather | solution.py:36
  49.9 5.4 %collective-permute-start.1 = (f32[3,128]{0,1:T(8,128)S(1)}, f32[3,128]{0,1:T(8,128)S(1)}, u32[]{:S(2)}, u32[]{:S(2)}) collective-permute-start(f32[3,128]{0,1:T(8,128)S(1)} %select_bitcast_fusion.3), channel_id=1, source_target_pairs={{0,508},{4,0},{8,4},{12,8},{16,12},{20,16},{24,20},{28,24},{32,28}... | collective-permute-start | bytes 4616 | tf_op jit(solution)/shard_map/ppermute | solution.py:17
  55.4 0.8 collective-permute-done.1
  56.2 1.9 collective-permute-start.2
  58.2 12.8 %collective-permute-done.2 = f32[3,128]{0,1:T(8,128)S(1)} collective-permute-done((f32[3,128]{0,1:T(8,128)S(1)}, f32[3,128]{0,1:T(8,128)S(1)}, u32[]{:S(2)}, u32[]{:S(2)}) %collective-permute-start.2) | collective-permute-done | bytes 1568 | tf_op jit(solution)/shard_map/ppermute | solution.py:17
  71.0 3.0 collective-permute-start.3
  74.1 1.9 collective-permute-done.3
  76.1 0.7 gather_fusion.8
  77.7 7.5 %broadcast_subtract_fusion = (f32[3,48,128,128]{3,2,1,0:T(8,128)}, f32[48,128,128]{2,1,0:T(8,128)}) fusion(f32[3,48,128]{2,1,0:T(8,128)S(1)} %copy.62, f32[3,48,128]{2,1,0:T(8,128)S(1)} %copy.61), kind=kLoop, calls=%fused_computation.19 | loop fusion | flops 6291456 | bytes 12730368 | tf_op jit(solution)/shard_map/sub | solution.py:29
  85.2 2.5 gather_fusion
  87.8 5.2 %fusion.21 = bf16[48,128,256]{2,1,0:T(8,128)(2,1)S(1)} fusion(bf16[48,256,256]{2,1,0:T(8,128)(2,1)} %gather_fusion.1, pred[48]{0:T(512)(128)(4,1)S(1)} %get-tuple-element.77, bf16[48,128,256]{2,1,0:T(8,128)(2,1)} %gather_fusion, pred[48]{0:T(512)(128)(4,1)S(1)} %get-tuple-element.76), kind=kOutput, calls=%fused_computation.42 | convolution fusion | flops 811597824 | bytes 12583008 | tf_op jit(solution)/shard_map/pbc,pcd->pbd/dot_general | solution.py:37
  93.0 1.0 fusion.80
  94.1 0.7 copy-done.3
  94.7 5.7 %fusion.2 = f32[2,128,256]{2,0,1:T(2,128)S(1)} fusion(f32[48,128,256]{2,1,0:T(8,128)S(1)} %fusion.80, s32[48]{0:T(128)S(1)} %copy-done.9), kind=kOutput, calls=%fused_computation.16 | convolution fusion | flops 37748832 | bytes 6553792 | tf_op jit(solution)/shard_map/so,oxe->sxe/dot_general | solution.py:94
  100.4 17.2 %all-reduce.7 = bf16[256,256]{1,0:T(8,128)(2,1)S(1)} all-reduce(f32[256,256]{1,0:T(8,128)S(1)} %bitcast.176), channel_id=1, replica_groups=mesh['dom'=128,'rep'=4] {'rep'}, use_global_device_ids=true, to_apply=%region_2.6 | all-reduce | flops 65536 | bytes 393216 | tf_op jit(solution)/shard_map/psum | solution.py:97
  118.2 2.6 gather_fusion.2
  120.8 10.7 %fusion.4 = f32[48,128,256]{2,1,0:T(8,128)} fusion(bf16[48,256,256]{2,1,0:T(8,128)(2,1)} %gather_fusion.1, pred[48]{0:T(512)(128)(4,1)S(1)} %get-tuple-element.77, bf16[48,128,256]{2,1,0:T(8,128)(2,1)} %gather_fusion.2, pred[48]{0:T(512)(128)(4,1)S(1)} %get-tuple-element.68, f32[48,128,128]{2,1,0:T(8,128)} %get-tuple-element.51, f32[48]{0:T(128)S(1)} %get-tuple-element.67), kind=kOutput, calls=%fused_computation.24 | convolution fusion | flops 1215823872 | bytes 18874656 | tf_op jit(solution)/shard_map/pbd,pcd->pbc/dot_general | solution.py:115
  131.6 8.3 %fusion = f32[6,128,256]{2,0,1:T(8,128)S(1)} fusion(f32[48,128,256]{2,1,0:T(8,128)} %fusion.4, s32[48]{0:T(128)S(1)} %copy-done.7), kind=kOutput, calls=%fused_computation.14 | convolution fusion | flops 113246496 | bytes 7078080 | tf_op jit(solution)/shard_map/jp,pbc->jbc/dot_general | solution.py:131
  140.4 0.9 fusion.57
  141.3 10.8 %fusion.10 = (f32[48,128,128]{2,1,0:T(8,128)S(1)}, f32[48,128,128]{2,1,0:T(8,128)}, f32[48,128,128]{2,1,0:T(8,128)}) fusion(f32[3,48,128,128]{3,2,1,0:T(8,128)} %get-tuple-element.50, bf16[48,128,256]{2,1,0:T(8,128)(2,1)} %copy-done.3, bf16[48,128,256]{2,1,0:T(8,128)(2,1)} %gather_fusion.2, pred[48]{0:T(512)(128)(4,1)S(1)} %get-tuple-element.68, ...), kind=kOutput, calls=%fused_computation.32 | convolution fusion | flops 408944640 | bytes 28311984 | tf_op jit(solution)/shard_map/pad,pbd->pab/dot_general | solution.py:109
  152.1 9.7 %fusion.30 = (f32[48,128]{1,0:T(8,128)S(1)}, f32[48,128]{1,0:T(8,128)S(1)}, f32[48,128]{1,0:T(8,128)S(1)}, f32[48,128]{1,0:T(8,128)S(1)}, f32[48,128]{1,0:T(8,12...) fusion(f32[48,128,128]{2,1,0:T(8,128)} %get-tuple-element.45, ...), kind=kLoop, calls=%fused_computation.49 | loop fusion | flops 18763776 | bytes 19316736 | tf_op jit(solution)/shard_map/reduce_sum | solution.py:127
  162.2 7.1 %collective-permute-start.12 = (f32[9,128]{1,0:T(8,128)S(1)}, f32[9,128]{1,0:T(8,128)S(1)}, u32[]{:S(2)}, u32[]{:S(2)}) collective-permute-start(f32[9,128]{1,0:T(8,128)S(1)} %get-tuple-element.52), channel_id=1, source_target_pairs={{0,508},{4,0},{8,4},{12,8},{16,12},{20,16},{24,20},{28,24},{32,28}... | collective-permute-start | bytes 13832 | tf_op jit(solution)/shard_map/ppermute | solution.py:17
  169.2 1.9 collective-permute-start.15
  171.2 6.7 %collective-permute-start.14 = (f32[9,128]{1,0:T(8,128)S(1)}, f32[9,128]{1,0:T(8,128)S(1)}, u32[]{:S(2)}, u32[]{:S(2)}) collective-permute-start(f32[9,128]{1,0:T(8,128)S(1)} %get-tuple-element.54), channel_id=1, source_target_pairs={{0,504},{4,508},{8,0},{12,4},{16,8},{20,12},{24,16},{28,20},{32,24... | collective-permute-start | bytes 13832 | tf_op jit(solution)/shard_map/ppermute | solution.py:17
  177.8 1.9 collective-permute-start.13
  180.2 1.9 collective-permute-start.9
  182.2 7.1 %collective-permute-start.10 = (f32[128,256]{1,0:T(8,128)S(1)}, f32[128,256]{1,0:T(8,128)S(1)}, u32[]{:S(2)}, u32[]{:S(2)}) collective-permute-start(f32[128,256]{1,0:T(8,128)S(1)} %bitcast.183), channel_id=1, source_target_pairs={{0,504},{4,508},{8,0},{12,4},{16,8},{20,12},{24,16},{28,20},{32,24... | collective-permute-start | bytes 393224 | tf_op jit(solution)/shard_map/ppermute | solution.py:17
  189.5 1.9 collective-permute-start.11
  191.7 2.7 collective-permute-start.8
  194.8 262.4 %all-reduce.6.cloned.1.call-done = f32[256,64]{1,0:T(8,128)} async-done(((f32[256,64]{1,0:T(8,128)}), f32[256,64]{1,0:T(8,128)}) %all-reduce.6.cloned.1.call-update) | async-done | bytes 65552
  457.2 1.2 constant_dynamic-slice_fusion
  460.1 17.0 %all-reduce.8 = (bf16[256,256]{1,0:T(8,128)(2,1)}, f32[9,256]{1,0:T(8,128)S(1)}) all-reduce(f32[256,256]{1,0:T(8,128)S(1)} %fusion.39, f32[9,256]{1,0:T(8,128)S(1)} %fusion.42), channel_id=1, replica_groups=mesh['dom'=128,'rep'=4] {'rep'}, use_global_device_ids=true, to_apply=%region_3.7 | all-reduce | flops 67840 | bytes 411648 | tf_op jit(solution)/shard_map/psum | solution.py:159
  (135 shorter events, 7.6 us)
Async XLA Ops:
  7.2 37.8 %copy-start = (bf16[8,256,256]{2,1,0:T(8,128)(2,1)S(1)}, bf16[8,256,256]{2,1,0:T(8,128)(2,1)}, u32[]{:S(2)}) copy-start(bf16[8,256,256]{2,1,0:T(8,128)(2,1)} %param.19) | copy-start | bytes 3145732
  7.2 33.4 %copy-start.6 = (s32[4,128]{1,0:T(4,128)S(1)}, s32[4,128]{1,0:T(4,128)}, u32[]{:S(2)}) copy-start(s32[4,128]{1,0:T(4,128)} %param.23) | copy-start | bytes 6148
  7.2 35.3 %copy-start.1 = (bf16[256,256]{1,0:T(8,128)(2,1)S(1)}, bf16[256,256]{1,0:T(8,128)(2,1)}, u32[]{:S(2)}) copy-start(bf16[256,256]{1,0:T(8,128)(2,1)} %param.17) | copy-start | bytes 393220
  7.2 35.7 %copy-start.5 = (f32[3,256]{1,0:T(4,128)S(1)}, f32[3,256]{1,0:T(4,128)}, u32[]{:S(2)}) copy-start(f32[3,256]{1,0:T(4,128)} %param.18) | copy-start | bytes 9220
  7.2 33.2 %copy-start.10 = (s32[48]{0:T(128)S(1)}, s32[48]{0:T(128)}, u32[]{:S(2)}) copy-start(s32[48]{0:T(128)} %param.26) | copy-start | bytes 580
  7.2 33.2 %copy-start.7 = (s32[48]{0:T(128)S(1)}, s32[48]{0:T(128)}, u32[]{:S(2)}) copy-start(s32[48]{0:T(128)} %param.25) | copy-start | bytes 580
  7.2 33.3 %copy-start.9 = (s32[48]{0:T(128)S(1)}, s32[48]{0:T(128)}, u32[]{:S(2)}) copy-start(s32[48]{0:T(128)} %param.24) | copy-start | bytes 580
  7.2 35.3 %copy-start.12 = (f32[8]{0:T(128)S(1)}, f32[8]{0:T(128)}, u32[]{:S(2)}) copy-start(f32[8]{0:T(128)} %param.22) | copy-start | bytes 100
  7.3 35.4 %copy-start.8 = (s32[3,48]{1,0:T(4,128)S(1)}, s32[3,48]{1,0:T(4,128)}, u32[]{:S(2)}) copy-start(s32[3,48]{1,0:T(4,128)} %param.27) | copy-start | bytes 1732
  7.3 450.0 %all-reduce.6.cloned.1.call-start = ((), (), s32[]{:S(2)}) async-start(), calls=%async_computation | async-start | bytes 262144
  9.9 75.3 %collective-permute-start.7 = (bf16[128,256]{1,0:T(8,128)(2,1)S(1)}, bf16[128,256]{1,0:T(8,128)(2,1)S(1)}, u32[]{:S(2)}, u32[]{:S(2)}) collective-permute-start(bf16[128,256]{1,0:T(8,128)(2,1)S(1)} %broadcast_select_fusion.9), channel_id=1, source_target_pairs={{0,504},{4,508},{8,0},{12,4},{16,8},{20,12},{24,16},{28,20},{32,24... | collective-permute-start | bytes 196616 | tf_op jit(solution)/shard_map/ppermute | solution.py:17
  25.9 59.3 %collective-permute-start.6 = (bf16[128,256]{1,0:T(8,128)(2,1)S(1)}, bf16[128,256]{1,0:T(8,128)(2,1)S(1)}, u32[]{:S(2)}, u32[]{:S(2)}) collective-permute-start(bf16[128,256]{1,0:T(8,128)(2,1)S(1)} %broadcast_select_fusion.10), channel_id=1, source_target_pairs={{0,8},{4,12},{8,16},{12,20},{16,24},{20,28},{24,32},{28,36},{32,40... | collective-permute-start | bytes 196616 | tf_op jit(solution)/shard_map/ppermute | solution.py:17
  29.6 55.6 %collective-permute-start.5 = (bf16[128,256]{1,0:T(8,128)(2,1)S(1)}, bf16[128,256]{1,0:T(8,128)(2,1)S(1)}, u32[]{:S(2)}, u32[]{:S(2)}) collective-permute-start(bf16[128,256]{1,0:T(8,128)(2,1)S(1)} %broadcast_select_fusion.11), channel_id=1, source_target_pairs={{0,508},{4,0},{8,4},{12,8},{16,12},{20,16},{24,20},{28,24},{32,28}... | collective-permute-start | bytes 196616 | tf_op jit(solution)/shard_map/ppermute | solution.py:17
  34.2 50.9 %collective-permute-start.4 = (bf16[128,256]{1,0:T(8,128)(2,1)S(1)}, bf16[128,256]{1,0:T(8,128)(2,1)S(1)}, u32[]{:S(2)}, u32[]{:S(2)}) collective-permute-start(bf16[128,256]{1,0:T(8,128)(2,1)S(1)} %broadcast_select_fusion.12), channel_id=1, source_target_pairs={{0,4},{4,8},{8,12},{12,16},{16,20},{20,24},{24,28},{28,32},{32,36}... | collective-permute-start | bytes 196616 | tf_op jit(solution)/shard_map/ppermute | solution.py:17
  38.5 11.4 %collective-permute-start = (f32[3,128]{0,1:T(8,128)S(1)}, f32[3,128]{0,1:T(8,128)S(1)}, u32[]{:S(2)}, u32[]{:S(2)}) collective-permute-start(f32[3,128]{0,1:T(8,128)S(1)} %select_bitcast_fusion.4), channel_id=1, source_target_pairs={{0,4},{4,8},{8,12},{12,16},{16,20},{20,24},{24,28},{28,32},{32,36}... | collective-permute-start | bytes 4616 | tf_op jit(solution)/shard_map/ppermute | solution.py:17
  49.9 6.2 %collective-permute-start.1 = (f32[3,128]{0,1:T(8,128)S(1)}, f32[3,128]{0,1:T(8,128)S(1)}, u32[]{:S(2)}, u32[]{:S(2)}) collective-permute-start(f32[3,128]{0,1:T(8,128)S(1)} %select_bitcast_fusion.3), channel_id=1, source_target_pairs={{0,508},{4,0},{8,4},{12,8},{16,12},{20,16},{24,20},{28,24},{32,28}... | collective-permute-start | bytes 4616 | tf_op jit(solution)/shard_map/ppermute | solution.py:17
  56.2 14.8 %collective-permute-start.2 = (f32[3,128]{0,1:T(8,128)S(1)}, f32[3,128]{0,1:T(8,128)S(1)}, u32[]{:S(2)}, u32[]{:S(2)}) collective-permute-start(f32[3,128]{0,1:T(8,128)S(1)} %select_bitcast_fusion.2), channel_id=1, source_target_pairs={{0,8},{4,12},{8,16},{12,20},{16,24},{20,28},{24,32},{28,36},{32,40... | collective-permute-start | bytes 4616 | tf_op jit(solution)/shard_map/ppermute | solution.py:17
  71.0 5.0 %collective-permute-start.3 = (f32[3,128]{0,1:T(8,128)S(1)}, f32[3,128]{0,1:T(8,128)S(1)}, u32[]{:S(2)}, u32[]{:S(2)}) collective-permute-start(f32[3,128]{0,1:T(8,128)S(1)} %select_bitcast_fusion.1), channel_id=1, source_target_pairs={{0,504},{4,508},{8,0},{12,4},{16,8},{20,12},{24,16},{28,20},{32,24... | collective-permute-start | bytes 4616 | tf_op jit(solution)/shard_map/ppermute | solution.py:17
  87.8 5.3 %copy-start.2 = (f32[48,128,128]{2,1,0:T(8,128)S(1)}, f32[48,128,128]{2,1,0:T(8,128)}, u32[]{:S(2)}) copy-start(f32[48,128,128]{2,1,0:T(8,128)} %get-tuple-element.51) | copy-start | bytes 9437188
  93.0 1.8 copy-start.3
  94.7 22.9 %copy-start.4 = (bf16[256,256]{1,0:T(8,128)(2,1)S(1)}, bf16[256,256]{1,0:T(8,128)(2,1)}, u32[]{:S(2)}) copy-start(bf16[256,256]{1,0:T(8,128)(2,1)} %param.20) | copy-start | bytes 393220
  94.7 22.9 %copy-start.11 = (f32[256]{0:T(256)S(1)}, f32[256]{0:T(256)}, u32[]{:S(2)}) copy-start(f32[256]{0:T(256)} %param.21) | copy-start | bytes 3076
  141.3 10.8 %slice-start = ((s8[9437184]{0:T(1024)(128)(4,1)}), s8[4194304]{0:T(1024)(128)(4,1)S(1)}, s32[]{:S(2)}) async-start(s8[9437184]{0:T(1024)(128)(4,1)} %bitcast.171), calls=%async_computation.1 | async-start | bytes 8388608
  141.3 10.8 %slice-start.1 = ((s8[9437184]{0:T(1024)(128)(4,1)}), s8[4194304]{0:T(1024)(128)(4,1)S(1)}, s32[]{:S(2)}) async-start(s8[9437184]{0:T(1024)(128)(4,1)} %bitcast.171), calls=%async_computation.2 | async-start | bytes 8388608
  141.3 10.8 %slice-start.2 = ((s8[9437184]{0:T(1024)(128)(4,1)}), s8[1048576]{0:T(1024)(128)(4,1)S(1)}, s32[]{:S(2)}) async-start(s8[9437184]{0:T(1024)(128)(4,1)} %bitcast.171), calls=%async_computation.3 | async-start | bytes 2097152
  162.2 32.4 %collective-permute-start.12 = (f32[9,128]{1,0:T(8,128)S(1)}, f32[9,128]{1,0:T(8,128)S(1)}, u32[]{:S(2)}, u32[]{:S(2)}) collective-permute-start(f32[9,128]{1,0:T(8,128)S(1)} %get-tuple-element.52), channel_id=1, source_target_pairs={{0,508},{4,0},{8,4},{12,8},{16,12},{20,16},{24,20},{28,24},{32,28}... | collective-permute-start | bytes 13832 | tf_op jit(solution)/shard_map/ppermute | solution.py:17
  169.2 12.9 %collective-permute-start.15 = (f32[9,128]{1,0:T(8,128)S(1)}, f32[9,128]{1,0:T(8,128)S(1)}, u32[]{:S(2)}, u32[]{:S(2)}) collective-permute-start(f32[9,128]{1,0:T(8,128)S(1)} %get-tuple-element.53), channel_id=1, source_target_pairs={{0,8},{4,12},{8,16},{12,20},{16,24},{20,28},{24,32},{28,36},{32,40... | collective-permute-start | bytes 13832 | tf_op jit(solution)/shard_map/ppermute | solution.py:17
  171.2 18.4 %collective-permute-start.14 = (f32[9,128]{1,0:T(8,128)S(1)}, f32[9,128]{1,0:T(8,128)S(1)}, u32[]{:S(2)}, u32[]{:S(2)}) collective-permute-start(f32[9,128]{1,0:T(8,128)S(1)} %get-tuple-element.54), channel_id=1, source_target_pairs={{0,504},{4,508},{8,0},{12,4},{16,8},{20,12},{24,16},{28,20},{32,24... | collective-permute-start | bytes 13832 | tf_op jit(solution)/shard_map/ppermute | solution.py:17
  177.8 13.8 %collective-permute-start.13 = (f32[9,128]{1,0:T(8,128)S(1)}, f32[9,128]{1,0:T(8,128)S(1)}, u32[]{:S(2)}, u32[]{:S(2)}) collective-permute-start(f32[9,128]{1,0:T(8,128)S(1)} %get-tuple-element.55), channel_id=1, source_target_pairs={{0,4},{4,8},{8,12},{12,16},{16,20},{20,24},{24,28},{28,32},{32,36}... | collective-permute-start | bytes 13832 | tf_op jit(solution)/shard_map/ppermute | solution.py:17
  180.2 278.3 %collective-permute-start.9 = (f32[128,256]{1,0:T(8,128)S(1)}, f32[128,256]{1,0:T(8,128)S(1)}, u32[]{:S(2)}, u32[]{:S(2)}) collective-permute-start(f32[128,256]{1,0:T(8,128)S(1)} %bitcast.184), channel_id=1, source_target_pairs={{0,4},{4,8},{8,12},{12,16},{16,20},{20,24},{24,28},{28,32},{32,36}... | collective-permute-start | bytes 393224 | tf_op jit(solution)/shard_map/ppermute | solution.py:17
  182.2 276.7 %collective-permute-start.10 = (f32[128,256]{1,0:T(8,128)S(1)}, f32[128,256]{1,0:T(8,128)S(1)}, u32[]{:S(2)}, u32[]{:S(2)}) collective-permute-start(f32[128,256]{1,0:T(8,128)S(1)} %bitcast.183), channel_id=1, source_target_pairs={{0,504},{4,508},{8,0},{12,4},{16,8},{20,12},{24,16},{28,20},{32,24... | collective-permute-start | bytes 393224 | tf_op jit(solution)/shard_map/ppermute | solution.py:17
  189.5 269.7 %collective-permute-start.11 = (f32[128,256]{1,0:T(8,128)S(1)}, f32[128,256]{1,0:T(8,128)S(1)}, u32[]{:S(2)}, u32[]{:S(2)}) collective-permute-start(f32[128,256]{1,0:T(8,128)S(1)} %bitcast.182), channel_id=1, source_target_pairs={{0,8},{4,12},{8,16},{12,20},{16,24},{20,28},{24,32},{28,36},{32,40... | collective-permute-start | bytes 393224 | tf_op jit(solution)/shard_map/ppermute | solution.py:17
  191.7 268.0 %collective-permute-start.8 = (f32[128,256]{1,0:T(8,128)S(1)}, f32[128,256]{1,0:T(8,128)S(1)}, u32[]{:S(2)}, u32[]{:S(2)}) collective-permute-start(f32[128,256]{1,0:T(8,128)S(1)} %bitcast.181), channel_id=1, source_target_pairs={{0,508},{4,0},{8,4},{12,8},{16,12},{20,16},{24,20},{28,24},{32,28}... | collective-permute-start | bytes 393224 | tf_op jit(solution)/shard_map/ppermute | solution.py:17
Sparse Core Ops, SparseCore 0:
  141.4 315.7 all-reduce.5
where the time goes:
time: 490 us; the launch traced here: 485 us
  waiting for transfers between devices  278 us (57%)
  starting transfers between devices  65.1 us (13%)
  matrix products  45.9 us (9%)
  blocking collectives  34.2 us (7%)
  local copies, waits for them, and re-layouts  27 us (6%)
  other arithmetic  19.1 us (4%)
  between operations  15.7 us (3%)
    unnamed x2, waiting for transfers between devices  262 us
    ppermute x16, starting transfers between devices, from_behind(): lax.ppermute(array, axis, [(i, (i + by) % count) for i in range(count)])  65.1 us
    psum x1, blocking collectives, on_device(): message = lax.psum(message_portion, 'rep')  17.2 us
    psum x1, blocking collectives, on_device(): totals = lax.psum((own_grad, self_side), 'rep')  17 us
    ppermute x16, waiting for transfers between devices, from_behind(): lax.ppermute(array, axis, [(i, (i + by) % count) for i in range(count)])  15.7 us
    dot_general x1, matrix products, on_device(): jnp.einsum('pad,pbd->pab', adjoint_tiles, mapped, preferred_element_type=...  10.8 us
    dot_general x1, matrix products, on_device(): jnp.einsum('pbd,pcd->pbc', mapped_grad, chosen, preferred_element_type=jn...  10.7 us
  transfers between devices with their start and end apart: 17, of which 4 were waited for; matrix products, arithmetic and copies ran while one was open for 10% of the time, Pallas kernels for 0%

commit v1 on v0

v1 whole, which is shorter than its diff:
```python
import functools

import jax
import jax.numpy as jnp
from jax import lax
from jax.experimental import pallas as pl
from jax.experimental.pallas import tpu as pltpu
from jax.sharding import PartitionSpec as P

TILE = 128
SLOTS = 3
QUAD = 4
SIDE = 16
OFFSETS = (1, -1, 2, -2)
EDGE = 2.0
FAR = 1.0e4
F32, BF16, I32 = jnp.float32, jnp.bfloat16, jnp.int32
COMPONENT_PAIRS = ((0, 0), (1, 1), (2, 2), (0, 1), (0, 2), (1, 2))

NN = (((1,), (0,)), ((), ()))
NT = (((1,), (1,)), ((), ()))
TN = (((0,), (0,)), ((), ()))


def dot(a, b, dims=NN):
    return lax.dot_general(a, b, dims, preferred_element_type=F32)


def iota(shape, dim):
    return lax.broadcasted_iota(I32, shape, dim)


def ones_where(mask, dtype=BF16):
    return jnp.where(mask, 1.0, 0.0).astype(dtype)


def split(x):
    high = x.astype(BF16).astype(F32)
    return high, (x - high).astype(BF16).astype(F32)


def pack_kernel(rows, feat, pos, home, other, kind, image, send, lists, pad, block):
    rep = lax.axis_index("rep")
    atoms = feat.shape[0]
    count = home.shape[1]
    pick = ones_where(iota((atoms, TILE), 0) == rows[pl.ds(rep, 1), :])
    send[0:TILE, :] = dot(pick, feat[...], TN).astype(BF16)
    pad[...] = jnp.zeros_like(pad)
    pad[0:3, :] = pos[...]
    whole = pad[...]
    high, mid = split(whole)
    low = whole - high - mid
    parts = jnp.concatenate([high, mid, low, jnp.zeros_like(low)], axis=0).astype(BF16)
    moved = dot(parts, pick).astype(BF16)
    send[TILE : TILE + SIDE, 0:TILE] = moved[0:SIDE]
    send[TILE : TILE + SIDE, TILE : 2 * TILE] = moved[SIDE : 2 * SIDE]
    block[...] = jnp.zeros_like(block)
    for q in range(4):

        @pl.when(rep == q)
        def _(q=q):
            span = slice(q * count, (q + 1) * count)
            block[0:1, span] = home[...]
            block[1:2, span] = other[...]
            block[2:3, span] = kind[...]
            block[3:6, span] = image[...]

    for q in range(4):
        lists[8 * q : 8 * q + 8, :] = block[...]


def plan_kernel(count, lists, plan):
    rep = lax.axis_index("rep")
    lanes = lists.shape[1]
    table = lists[0:8, :] + lists[8:16, :] + lists[16:24, :] + lists[24:32, :]
    home, other = table[0:1, :], table[1:2, :]
    valid = jnp.where(iota((1, lanes), 1) < 4 * count, 1, 0)
    ahead = ones_where(iota((lanes, lanes), 0) < iota((lanes, lanes), 1))

    def before(first, second):
        both = jnp.where(iota((16, lanes), 0) < 8, first, second)
        found = dot(both.astype(F32).astype(BF16), ahead).astype(I32)
        return found[0:1, :], found[8:9, :]

    def total(x):
        return jnp.sum(x.astype(F32), axis=1, keepdims=True).astype(I32)

    local = jnp.where(other < 2, valid, 0)
    start = jnp.zeros((1, 1), I32)
    quota = jnp.zeros((1, 1), I32)
    for q in range(4):
        room = jnp.maximum(count - total(jnp.where(other == 2 + q, valid, 0)), 0)
        start = start + jnp.where(q < rep, room, 0)
        quota = quota + jnp.where(q == rep, room, 0)
    turn, _ = before(local, local)
    taken = jnp.where(turn >= start, local, 0) * jnp.where(turn < start + quota, 1, 0)
    mine = taken + jnp.where(other == 2 + rep, valid, 0)
    first = jnp.where(home == 0, mine, 0)
    second = mine - first
    place_first, place_second = before(first, second)
    quads_first = (total(first) + (QUAD - 1)) // QUAD
    quads_second = (total(second) + (QUAD - 1)) // QUAD
    place = jnp.where(first > 0, place_first, place_second + quads_first * QUAD)
    place = jnp.where(mine > 0, place, -1)
    put = ones_where(iota((lanes, lanes), 0) == place)
    row = iota((8, lanes), 0)
    fields = jnp.where(row == 1, jnp.minimum(table, 2), table)
    fields = jnp.where(row == 6, 1, fields).astype(F32)
    fields = jnp.concatenate([fields, jnp.zeros_like(fields)], axis=0).astype(BF16)
    listed = dot(fields, put, NT)[0:8, :].astype(I32)
    plan[...] = jnp.where(row == 7, quads_first + quads_second, listed)


def place_coordinates(pos, halo, rows, columns):
    rows[...] = jnp.zeros_like(rows)
    for t in range(2):
        rows[t, 0:3, :] = pos[:, t * TILE : (t + 1) * TILE]
    side = halo[TILE : TILE + SIDE, :].astype(F32)
    rows[2] = side[0:8, 0:TILE] + side[8:16, 0:TILE] + side[0:8, TILE : 2 * TILE]
    for t in range(2):
        block = rows[t]
        for c in range(3):
            columns[t * 3 + c] = jnp.transpose(jnp.broadcast_to(block[c : c + 1, :], (TILE, TILE)))


def pair_fields(plan, decay, p):
    slot, kind = plan[1, p], plan[2, p]
    shift = [plan[3 + c, p].astype(F32) * EDGE for c in range(3)]
    away = (1 - plan[6, p]).astype(F32) * FAR
    return slot, kind, shift, away, decay[kind]


def radial_kernel(rows, columns, home, slot, shift, away, rate):
    partner = rows[slot]
    square = None
    for c in range(3):
        by = shift[c] + away if c == 0 else shift[c]
        apart = (partner[c : c + 1, :] + by) - columns[home * 3 + c]
        square = apart * apart if square is None else square + apart * apart
    return jnp.exp(square * (-rate))


def tile_of(slot):
    return pl.ds(pl.multiple_of(slot * TILE, TILE), TILE)


def forward_kernel(plan, decay, feat, pos, halo, radial, mapped, partial, rows, columns, message):
    place_coordinates(pos, halo, rows, columns)
    atoms = feat.shape[0]
    for k in range(radial.shape[0]):
        mapped[k, 0:atoms, :] = dot(feat[...], radial[k]).astype(BF16)
        mapped[k, atoms : atoms + TILE, :] = dot(halo[0:TILE, :], radial[k]).astype(BF16)
    message[...] = jnp.zeros_like(message)

    def quad(q, carry):
        home = plan[0, q * QUAD]
        total = None
        for u in range(QUAD):
            slot, kind, shift, away, rate = pair_fields(plan, decay, q * QUAD + u)
            kernel = radial_kernel(rows, columns, home, slot, shift, away, rate).astype(BF16)
            part = dot(kernel, mapped[kind, tile_of(slot), :])
            total = part if total is None else total + part
        message[home] += total
        return carry

    lax.fori_loop(0, plan[7, 0], quad, 0)
    for t in range(2):
        low = message[t].astype(BF16)
        for q in range(4):
            partial[q * atoms + t * TILE : q * atoms + (t + 1) * TILE, :] = low


def backward_kernel(
    plan, decay, partial, mixing, readout, pos, halo, radial, mapped,
    back, own_grad, own_side, mixing_part,
    rows, columns, adjoint, flipped, turned, bases, sums, side,
):
    rep = lax.axis_index("rep")
    atoms, channels = own_grad.shape
    place_coordinates(pos, halo, rows, columns)
    message = partial[0:atoms, :].astype(F32)
    for q in range(1, 4):
        message = message + partial[q * atoms : (q + 1) * atoms, :].astype(F32)
    packed = message.astype(BF16)
    mixed = dot(packed, mixing[...])
    gate = jax.nn.sigmoid(mixed)
    slope = (readout[...] * gate * (1.0 + mixed * (1.0 - gate))).astype(BF16)
    adjoint[...] = dot(slope, mixing[...], NT).astype(BF16).reshape(2, TILE, channels)
    for t in range(2):
        flipped[t] = dot(mixing[...], slope[t * TILE : (t + 1) * TILE, :], NT).astype(BF16)

    half = channels // 2
    share = channels // 4
    gradient = None
    for odd in range(2):
        take_rows = ones_where(iota((channels, half), 0) == 2 * iota((channels, half), 1) + odd)
        lane = iota((channels, TILE), 1) - odd * share
        inside = jnp.where(lane >= 0, 1, 0) * jnp.where(lane < share, 1, 0)
        take_cols = ones_where(jnp.where(inside > 0, lane + rep * share, -1) == iota((channels, TILE), 0))
        left = dot(packed, take_rows).astype(BF16)
        right = dot(slope, take_cols).astype(BF16)
        part = dot(left, right, TN)
        gradient = part if gradient is None else gradient + part
    mixing_part[...] = gradient

    row = iota((SIDE, TILE), 0)

    def marks(*which):
        found = jnp.zeros((SIDE, TILE), F32)
        for r in which:
            found = jnp.where(row == r, 1.0, found)
        return found

    left_marks = (marks(1, 4, 8, 9), marks(2, 5, 10), marks(3, 6))
    right_marks = (marks(4), marks(5, 8), marks(6, 9, 10))
    left_one, right_one = marks(0), marks(0, 1, 2, 3)
    for t in range(SLOTS):
        block = rows[t]
        left, right = left_one, right_one
        for c in range(3):
            left = left + left_marks[c] * block[c : c + 1, :]
            right = right + right_marks[c] * block[c : c + 1, :]
        bases[t, 0:SIDE, :] = left
        bases[t, SIDE : 2 * SIDE, :] = right
    sums[...] = jnp.zeros_like(sums)
    turned[...] = jnp.zeros_like(turned)

    def monomials(t, left_shift, right_shift):
        base = bases[t]
        high, low = split((base[0:SIDE] + left_shift) * (base[SIDE : 2 * SIDE] + right_shift))
        both = jnp.concatenate([high, low], axis=0).astype(BF16)
        return jnp.concatenate([both, both], axis=1)

    def quad(q, carry):
        home = plan[0, q * QUAD]
        home_sum = None
        for u in range(QUAD):
            slot, kind, shift, away, rate = pair_fields(plan, decay, q * QUAD + u)
            kernel = radial_kernel(rows, columns, home, slot, shift, away, rate)
            pull = dot(adjoint[home], mapped[kind, tile_of(slot), :], NT)
            weight = (kernel * (-2.0 * rate)) * pull
            high = weight.astype(BF16)
            low = (weight - high.astype(F32)).astype(BF16)
            left_shift = sum(left_marks[c] * shift[c] for c in range(3))
            right_shift = sum(right_marks[c] * shift[c] for c in range(3))
            far = monomials(slot, left_shift, right_shift)
            near = monomials(home, -left_shift, -right_shift)
            part = dot(far, jnp.concatenate([high, low], axis=1), NT)
            home_sum = part if home_sum is None else home_sum + part
            sums[slot] += dot(near, jnp.concatenate([high, low], axis=0))
            turned[kind * SLOTS + slot] += dot(flipped[home], kernel.astype(BF16))
        sums[home] += home_sum
        return carry

    lax.fori_loop(0, plan[7, 0], quad, 0)

    side[...] = jnp.zeros_like(side)
    for t in range(SLOTS):
        found = sums[t]
        found = found[0:SIDE] + found[SIDE : 2 * SIDE]
        at = [rows[t][c : c + 1, :] for c in range(3)]
        zeroth = found[0:1, :]
        once = [found[1 + c : 2 + c, :] for c in range(3)]
        for c in range(3):
            side[t, c : c + 1, :] = once[c] - at[c] * zeroth
        for n, (a, b) in enumerate(COMPONENT_PAIRS):
            at_row = 4 + n if n < 3 else 5 + n
            twice = found[at_row : at_row + 1, :]
            side[t, 8 + n : 9 + n, :] = -0.5 * (
                twice - at[b] * once[a] - at[a] * once[b] + at[a] * at[b] * zeroth
            )
        total = None
        for k in range(radial.shape[0]):
            part = dot(radial[k], turned[k * SLOTS + t].astype(BF16))
            total = part if total is None else total + part
        gradient = jnp.transpose(total)
        if t < 2:
            own_grad[t * TILE : (t + 1) * TILE, :] = gradient
            own_side[:, t * TILE : (t + 1) * TILE] = side[t]
        else:
            back[0:TILE, :] = gradient.astype(BF16)
            high, low = split(side[t])
            back[TILE : TILE + SIDE, 0:TILE] = high.astype(BF16)
            back[TILE : TILE + SIDE, TILE : 2 * TILE] = low.astype(BF16)


def return_kernel(rows, got, own_grad, own_side, payload):
    rep = lax.axis_index("rep")
    atoms = own_grad.shape[0]
    pick = ones_where(iota((atoms, TILE), 0) == rows[pl.ds(rep, 1), :])
    grad = (own_grad[...] + dot(pick, got[0:TILE, :])).astype(BF16)
    came = got[TILE : TILE + SIDE, :]
    side = own_side[...] + dot(came[:, 0:TILE], pick, NT) + dot(came[:, TILE : 2 * TILE], pick, NT)
    high, low = split(side)
    both = jnp.concatenate([high, low], axis=0).astype(BF16)
    height = atoms + 2 * SIDE
    for q in range(4):
        payload[q * height : q * height + atoms, :] = grad
        payload[q * height + atoms : (q + 1) * height, :] = both


def final_kernel(payload, mixing_parts, grad, forces, virials, grad_mixing):
    atoms = grad.shape[0]
    height = atoms + 2 * SIDE
    total = None
    side = None
    for q in range(4):
        part = payload[q * height : q * height + atoms, :].astype(F32)
        total = part if total is None else total + part
        both = payload[q * height + atoms : (q + 1) * height, :].astype(F32)
        part = both[0:SIDE] + both[SIDE : 2 * SIDE]
        side = part if side is None else side + part
    grad[...] = total.astype(BF16)
    forces[...] = side[0:3]
    virials[...] = side[8:14]
    found = jnp.sum(mixing_parts[...], axis=0, keepdims=True)
    share = grad_mixing.shape[1]
    grad_mixing[0:1, :] = found[:, 0:share]
    grad_mixing[1:2, :] = found[:, share : 2 * share]


def call(kernel, outs, ins, scratch=(), scalars=0, flops=0, moved=1 << 20):
    vmem = pl.BlockSpec(memory_space=pltpu.VMEM)
    smem = pl.BlockSpec(memory_space=pltpu.SMEM)
    return pl.pallas_call(
        kernel,
        out_shape=[jax.ShapeDtypeStruct(shape, dtype) for shape, dtype in outs],
        in_specs=[smem] * scalars + [vmem] * (len(ins) - scalars),
        out_specs=[vmem] * len(outs),
        scratch_shapes=[pltpu.VMEM(shape, dtype) for shape, dtype in scratch],
        compiler_params=pltpu.CompilerParams(vmem_limit_bytes=40 << 20),
        cost_estimate=pl.CostEstimate(flops=flops, bytes_accessed=moved, transcendentals=0),
    )(*ins)


def on_device(
    features, positions, radial, mixing, readout, decay,
    send_rows, pair_home, pair_other, pair_kind, pair_image,
):
    atoms, channels = features.shape
    kinds = radial.shape[0]
    count = pair_home.shape[0]
    doms, reps = lax.axis_size("dom"), lax.axis_size("rep")
    lanes = 2 * TILE
    assert reps == len(OFFSETS) and atoms == 2 * TILE and 4 * count <= lanes - 64

    def hop(array, sign):
        ways = [
            (d * reps + r, (d + sign * OFFSETS[r]) % doms * reps + r)
            for d in range(doms)
            for r in range(reps)
        ]
        return lax.ppermute(array, ("dom", "rep"), ways)

    send, lists = call(
        pack_kernel,
        [((TILE + SIDE, channels), BF16), ((32, lanes), I32)],
        [send_rows, features, positions]
        + [x.reshape(1, count) for x in (pair_home, pair_other, pair_kind)]
        + [pair_image],
        [((8, atoms), F32), ((8, lanes), I32)],
        flops=1 << 24,
    )
    halo = hop(send, 1)
    lists = lax.all_to_all(lists, "rep", 0, 0, tiled=True)
    [plan] = call(functools.partial(plan_kernel, count), [((8, lanes), I32)], [lists], flops=1 << 20)

    coordinates = [((SLOTS, 8, TILE), F32), ((6, TILE, TILE), F32)]
    mapped, partial = call(
        forward_kernel,
        [((kinds, SLOTS * TILE, channels), BF16), ((reps * atoms, channels), BF16)],
        [plan, decay, features, positions, halo, radial],
        coordinates + [((2, TILE, channels), F32)],
        scalars=2,
        flops=1 << 30,
    )
    partial = lax.all_to_all(partial, "rep", 0, 0, tiled=True)
    back, own_grad, own_side, mixing_part = call(
        backward_kernel,
        [
            ((TILE + SIDE, channels), BF16),
            ((atoms, channels), F32),
            ((SIDE, atoms), F32),
            ((channels // 2, TILE), F32),
        ],
        [plan, decay, partial, mixing, readout.reshape(1, channels), positions, halo, radial, mapped],
        coordinates
        + [
            ((2, TILE, channels), BF16),
            ((2, channels, TILE), BF16),
            ((kinds * SLOTS, channels, TILE), F32),
            ((SLOTS, 2 * SIDE, TILE), F32),
            ((SLOTS, 2 * SIDE, TILE), F32),
            ((SLOTS, SIDE, TILE), F32),
        ],
        scalars=2,
        flops=1 << 31,
    )
    got = hop(back, -1)
    rows_each = channels // 2 // doms
    mixing_parts = lax.all_to_all(mixing_part, "dom", 0, 0, tiled=True)
    height = atoms + 2 * SIDE
    [payload] = call(
        return_kernel,
        [((reps * height, channels), BF16)],
        [send_rows, got, own_grad, own_side],
        flops=1 << 24,
    )
    payload = lax.all_to_all(payload, "rep", 0, 0, tiled=True)
    return tuple(
        call(
            final_kernel,
            [
                ((atoms, channels), BF16),
                ((3, atoms), F32),
                ((6, atoms), F32),
                ((2 * rows_each, channels // reps), F32),
            ],
            [payload, mixing_parts],
            flops=1 << 20,
        )
    )


def solution(mesh):
    in_specs = (
        P("dom", None),
        P(None, "dom"),
        P(),
        P(),
        P(),
        P(),
        P(None, "dom"),
        P(("dom", "rep")),
        P(("dom", "rep")),
        P(("dom", "rep")),
        P(None, ("dom", "rep")),
    )
    out_specs = (P("dom", None), P(None, "dom"), P(None, "dom"), P("dom", "rep"))
    return jax.shard_map(
        on_device, mesh=mesh, in_specs=in_specs, out_specs=out_specs, check_vma=False
    )
```

time: 490 us -> 98.7 us (0.20)
  waiting for transfers between devices: 278 us -> 11.8 us
  matrix products: 45.9 us -> 0 us
  starting transfers between devices: 65.1 us -> 19.4 us
  Pallas kernels: 0 us -> 19.4 us
  local copies, waits for them, and re-layouts: 27 us -> 7.73 us
  other arithmetic: 19.1 us -> 0 us
  between operations: 15.7 us -> 0.76 us
    unnamed x2 -> x0, waiting for transfers between devices: 262 us -> none
    ppermute x16 -> x2, starting transfers between devices: 65.1 us -> 7.31 us  [hop(): return lax.ppermute(array, ('dom', 'rep'), ways)]
    dot_general x19 -> x0, matrix products: 45.9 us -> none  [the longest x1 10.8 us: on_device(): jnp.einsum('pad,pbd->pab', adjoint_tiles, mapped, preferred_element_type=...]
    all_to_all x0 -> x3, blocking collectives: none -> 39.1 us  [the longest x1 17.8 us: on_device(): lists = lax.all_to_all(lists, 'rep', 0, 0, tiled=True)]
    psum x2 -> x0, blocking collectives: 34.2 us -> none  [the longest x1 17.2 us: on_device(): message = lax.psum(message_portion, 'rep')]
    gather x13 -> x0, local copies, waits for them, and re-layouts: 20.6 us -> none  [the longest x4 6.72 us: on_device(): picked_feat = jnp.take(features, send_rows[section_no], axis=0)]
    pallas_call x0 -> x6, Pallas kernels: none -> 19.4 us  [call(): pl.pallas_call(kernel, out_shape=[jax.ShapeDtypeStruct(shape, dtype) for...]
    ppermute x16 -> x2, waiting for transfers between devices: 15.7 us -> 3.23 us  [hop(): return lax.ppermute(array, ('dom', 'rep'), ways)]
  transfers between devices with their start and end apart: 17 -> 3, of which waited for: 4 -> 2; matrix products, arithmetic and copies ran while one was open for 10% -> 0% of each run, Pallas kernels for 0% -> 1%
where the time goes in v1:
time: 98.7 us; the launch traced here: 98.2 us
  blocking collectives  39.1 us (40%)
  Pallas kernels  19.4 us (20%)
  starting transfers between devices  19.4 us (20%)
  waiting for transfers between devices  11.8 us (12%)
  local copies, waits for them, and re-layouts  7.73 us (8%)
    pallas_call x6, Pallas kernels, call(): pl.pallas_call(kernel, out_shape=[jax.ShapeDtypeStruct(shape, dtype) for...  19.4 us
    all_to_all x1, blocking collectives, on_device(): lists = lax.all_to_all(lists, 'rep', 0, 0, tiled=True)  17.8 us
    all_to_all x1, starting transfers between devices, on_device(): mixing_parts = lax.all_to_all(mixing_part, 'dom', 0, 0, tiled=True)  12.1 us
    all_to_all x1, blocking collectives, on_device(): payload = lax.all_to_all(payload, 'rep', 0, 0, tiled=True)  12 us
    all_to_all x1, blocking collectives, on_device(): partial = lax.all_to_all(partial, 'rep', 0, 0, tiled=True)  9.36 us
    all_to_all x1, waiting for transfers between devices, on_device(): mixing_parts = lax.all_to_all(mixing_part, 'dom', 0, 0, tiled=True)  8.58 us
    unnamed x32, local copies, waits for them, and re-layouts  7.73 us
    ppermute x2, starting transfers between devices, hop(): return lax.ppermute(array, ('dom', 'rep'), ways)  7.31 us
  transfers between devices with their start and end apart: 3, of which 2 were waited for; matrix products, arithmetic and copies ran while one was open for 0% of the time, Pallas kernels for 1%

profile of v1, /device:TPU:1, one launch (start us, length us, event | category | flops | bytes accessed | tf_op | source)
XLA Modules:
  0.0 98.2 jit_solution(3291459311889271813)
XLA Ops:
  0.6 0.0 copy-start
  0.6 0.9 copy-done
  1.5 0.0 copy-start.2
  1.5 0.7 copy-done.2
  2.2 0.0 copy-start.4
  2.2 0.7 copy-done.4
  2.9 0.0 copy-start.6
  2.9 0.7 copy-done.6
  3.6 0.0 copy-start.7
  3.6 0.7 copy-done.7
  4.2 0.0 copy-start.8
  4.2 0.7 copy-done.8
  4.9 0.0 copy-start.9
  4.9 0.7 copy-done.9
  5.6 0.2 shard_map.138
  5.8 4.5 %collective-permute-start = (bf16[144,256]{1,0:T(8,128)(2,1)S(1)}, bf16[144,256]{1,0:T(8,128)(2,1)S(1)}, u32[]{:S(2)}, u32[]{:S(2)}) collective-permute-start(bf16[144,256]{1,0:T(8,128)(2,1)S(1)} %get-tuple-element.13), channel_id=1, source_target_pairs={{0,4},{1,509},{2,10},{3,507},{4,8},{5,1},{6,14},{7,511},{8,12},{9,... | collective-permute-start | bytes 221192 | tf_op jit(solution)/shard_map/ppermute | solution.py:353
  10.3 17.8 %all_to_all.44 = s32[4,8,256]{2,1,0:T(8,128)S(1)} all-to-all(s32[4,8,256]{2,1,0:T(8,128)S(1)} %bitcast.20), channel_id=1, replica_groups=mesh['dom'=128,'rep'=4] {'rep'}, dimensions={0} | all-to-all | bytes 65536 | tf_op jit(solution)/shard_map/all_to_all | solution.py:365
  28.1 0.4 shard_map.139.plan
  28.6 0.0 collective-permute-done.halo
  28.6 0.0 copy-start.1
  28.6 0.9 copy-done.1
  29.5 0.0 copy-start.10
  29.5 1.2 %copy-done.10 = bf16[8,256,256]{2,1,0:T(8,128)(2,1)S(1)} copy-done((bf16[8,256,256]{2,1,0:T(8,128)(2,1)S(1)}, bf16[8,256,256]{2,1,0:T(8,128)(2,1)}, u32[]{:S(2)}) %copy-start.10) | copy-done | bytes 1048600
  30.7 0.0 copy-start.14
  30.7 0.7 copy-done.14
  31.4 0.0 copy-start.5
  31.4 0.0 copy-start.11
  31.4 0.0 copy-start.12
  31.4 0.0 copy-start.13
  31.4 0.0 copy-start.15
  31.4 4.7 %shard_map.140 = (bf16[8,384,256]{2,1,0:T(8,128)(2,1)S(1)}, bf16[1024,256]{1,0:T(8,128)(2,1)S(1)}) custom-call(s32[8,256]{1,0:T(8,128)S(1)} %shard_map.139.plan, f32[8]{0:T(128)S(1)} %copy-done.14, bf16[256,256]{1,0:T(8,128)(2,1)S(1)} %copy-done.1, f32[3,256]{1,0:T(4,128)S(1)} %copy-done.4, bf16[144,256]{1,0:T(8,128)(2,1)S(1)} %collective-permute-done.halo, ...), custom_call_target="tpu_custom_call" | custom-call | flops 1073741824 | bytes 1048576 | tf_op jit(solution)/shard_map/pallas_call | solution.py:325
  36.1 9.4 %all_to_all.45 = bf16[4,256,256]{2,1,0:T(8,128)(2,1)S(1)} all-to-all(bf16[4,256,256]{2,1,0:T(8,128)(2,1)S(1)} %bitcast.17), channel_id=1, replica_groups=mesh['dom'=128,'rep'=4] {'rep'}, dimensions={0} | all-to-all | bytes 1048576 | tf_op jit(solution)/shard_map/all_to_all | solution.py:377
  45.5 0.0 copy-done.5
  45.5 0.0 copy-done.11
  45.5 0.0 copy-done.12
  45.5 0.0 copy-done.13
  45.5 0.0 copy-done.15
  45.5 0.0 copy-start.3
  45.5 13.1 %shard_map.141 = (bf16[144,256]{1,0:T(8,128)(2,1)S(1)}, f32[256,256]{1,0:T(8,128)S(1)}, f32[16,256]{1,0:T(8,128)S(1)}, f32[128,128]{1,0:T(8,128)}) custom-call(s32[8,256]{1,0:T(8,128)S(1)} %shard_map.139.plan, f32[8]{0:T(128)S(1)} %copy-done.15, bf16[1024,256]{1,0:T(8,128)(2,1)S(1)} %bitcast.16, bf16[256,256]{1,0:T(8,128)(2,1)S(1)} %copy-done.12, ...), custom_call_target="tpu_custom_call" | custom-call | flops 2147483648 | bytes 1048576 | tf_op jit(solution)/shard_map/pallas_call | solution.py:325
  58.6 12.1 %all-to-all-start.3 = ((f32[128,1,128]{2,1,0:T(1,128)}), f32[128,1,128]{2,1,0:T(1,128)S(1)}, u32[]{:S(2)}, u32[]{:S(2)}) async-start(f32[128,1,128]{2,1,0:T(1,128)} %bitcast.11), calls=%async_computation.3 | async-start | bytes 131072 | tf_op jit(solution)/shard_map/all_to_all | solution.py:401
  70.7 2.8 %collective-permute-start.1 = (bf16[144,256]{1,0:T(8,128)(2,1)S(1)}, bf16[144,256]{1,0:T(8,128)(2,1)S(1)}, u32[]{:S(2)}, u32[]{:S(2)}) collective-permute-start(bf16[144,256]{1,0:T(8,128)(2,1)S(1)} %get-tuple-element.16), channel_id=1, source_target_pairs={{0,508},{1,5},{2,506},{3,11},{4,0},{5,9},{6,510},{7,15},{8,4},{9,1... | collective-permute-start | bytes 221192 | tf_op jit(solution)/shard_map/ppermute | solution.py:353
  73.5 3.2 %collective-permute-done.1.got = bf16[144,256]{1,0:T(8,128)(2,1)S(1)} collective-permute-done((bf16[144,256]{1,0:T(8,128)(2,1)S(1)}, bf16[144,256]{1,0:T(8,128)(2,1)S(1)}, u32[]{:S(2)}, u32[]{:S(2)}) %collective-permute-start.1) | collective-permute-done | bytes 73760 | tf_op jit(solution)/shard_map/ppermute | solution.py:353
  76.7 0.0 copy-done.3
  76.7 0.2 shard_map.142
  76.9 8.6 %all-to-all-done.3 = f32[128,1,128]{2,1,0:T(1,128)S(1)} async-done(((f32[128,1,128]{2,1,0:T(1,128)}), f32[128,1,128]{2,1,0:T(1,128)S(1)}, u32[]{:S(2)}, u32[]{:S(2)}) %all-to-all-start.3) | async-done | bytes 65568 | tf_op jit(solution)/shard_map/all_to_all | solution.py:401
  85.5 12.0 %all_to_all.46 = bf16[4,288,256]{2,1,0:T(8,128)(2,1)S(1)} all-to-all(bf16[4,288,256]{2,1,0:T(8,128)(2,1)S(1)} %bitcast.14), channel_id=1, replica_groups=mesh['dom'=128,'rep'=4] {'rep'}, dimensions={0} | all-to-all | bytes 1179648 | tf_op jit(solution)/shard_map/all_to_all | solution.py:409
  97.4 0.8 shard_map.143
Async XLA Ops:
  0.6 0.9 copy-start
  1.5 0.7 copy-start.2
  2.2 0.7 copy-start.4
  2.9 0.7 copy-start.6
  3.6 0.7 copy-start.7
  4.2 0.7 copy-start.8
  4.9 0.7 copy-start.9
  5.8 22.8 %collective-permute-start = (bf16[144,256]{1,0:T(8,128)(2,1)S(1)}, bf16[144,256]{1,0:T(8,128)(2,1)S(1)}, u32[]{:S(2)}, u32[]{:S(2)}) collective-permute-start(bf16[144,256]{1,0:T(8,128)(2,1)S(1)} %get-tuple-element.13), channel_id=1, source_target_pairs={{0,4},{1,509},{2,10},{3,507},{4,8},{5,1},{6,14},{7,511},{8,12},{9,... | collective-permute-start | bytes 221192 | tf_op jit(solution)/shard_map/ppermute | solution.py:353
  28.6 0.9 copy-start.1
  29.5 1.2 %copy-start.10 = (bf16[8,256,256]{2,1,0:T(8,128)(2,1)S(1)}, bf16[8,256,256]{2,1,0:T(8,128)(2,1)}, u32[]{:S(2)}) copy-start(bf16[8,256,256]{2,1,0:T(8,128)(2,1)} %radial.3) | copy-start | bytes 3145732
  30.7 0.7 copy-start.14
  31.4 14.1 %copy-start.5 = (f32[3,256]{1,0:T(4,128)S(1)}, f32[3,256]{1,0:T(4,128)}, u32[]{:S(2)}) copy-start(f32[3,256]{1,0:T(4,128)} %pos.5) | copy-start | bytes 9220
  31.4 14.1 %copy-start.11 = (bf16[8,256,256]{2,1,0:T(8,128)(2,1)S(1)}, bf16[8,256,256]{2,1,0:T(8,128)(2,1)}, u32[]{:S(2)}) copy-start(bf16[8,256,256]{2,1,0:T(8,128)(2,1)} %radial.3) | copy-start | bytes 3145732
  31.4 14.1 %copy-start.12 = (bf16[256,256]{1,0:T(8,128)(2,1)S(1)}, bf16[256,256]{1,0:T(8,128)(2,1)}, u32[]{:S(2)}) copy-start(bf16[256,256]{1,0:T(8,128)(2,1)} %mixing.1) | copy-start | bytes 393220
  31.4 14.1 %copy-start.13 = (f32[256]{0:T(256)S(1)}, f32[256]{0:T(256)}, u32[]{:S(2)}) copy-start(f32[256]{0:T(256)} %param.15) | copy-start | bytes 3076
  31.4 14.1 %copy-start.15 = (f32[8]{0:T(128)S(1)}, f32[8]{0:T(128)}, u32[]{:S(2)}) copy-start(f32[8]{0:T(128)} %decay.3) | copy-start | bytes 100
  45.5 31.2 %copy-start.3 = (s32[4,128]{1,0:T(4,128)S(1)}, s32[4,128]{1,0:T(4,128)}, u32[]{:S(2)}) copy-start(s32[4,128]{1,0:T(4,128)} %rows.3) | copy-start | bytes 6148
  58.6 26.9 %all-to-all-start.3 = ((f32[128,1,128]{2,1,0:T(1,128)}), f32[128,1,128]{2,1,0:T(1,128)S(1)}, u32[]{:S(2)}, u32[]{:S(2)}) async-start(f32[128,1,128]{2,1,0:T(1,128)} %bitcast.11), calls=%async_computation.3 | async-start | bytes 131072 | tf_op jit(solution)/shard_map/all_to_all | solution.py:401
  70.7 6.0 %collective-permute-start.1 = (bf16[144,256]{1,0:T(8,128)(2,1)S(1)}, bf16[144,256]{1,0:T(8,128)(2,1)S(1)}, u32[]{:S(2)}, u32[]{:S(2)}) collective-permute-start(bf16[144,256]{1,0:T(8,128)(2,1)S(1)} %get-tuple-element.16), channel_id=1, source_target_pairs={{0,508},{1,5},{2,506},{3,11},{4,0},{5,9},{6,510},{7,15},{8,4},{9,1... | collective-permute-start | bytes 221192 | tf_op jit(solution)/shard_map/ppermute | solution.py:353

commit v2 on v1

v2 whole, which is shorter than its diff:
```python
import functools

import jax
import jax.numpy as jnp
from jax import lax
from jax.experimental import pallas as pl
from jax.experimental.pallas import tpu as pltpu
from jax.sharding import PartitionSpec as P

TILE = 128
SLOTS = 3
QUAD = 8
SIDE = 16
OFFSETS = (1, -1, 2, -2)
EDGE = 2.0
FAR = 1.0e4
DEPTH = 64
F32, BF16, I32 = jnp.float32, jnp.bfloat16, jnp.int32
COMPONENT_PAIRS = ((0, 0), (1, 1), (2, 2), (0, 1), (0, 2), (1, 2))

NN = (((1,), (0,)), ((), ()))
NT = (((1,), (1,)), ((), ()))
TN = (((0,), (0,)), ((), ()))


def dot(a, b, dims=NN):
    return lax.dot_general(a, b, dims, preferred_element_type=F32)


def iota(shape, dim):
    return lax.broadcasted_iota(I32, shape, dim)


def ones_where(mask, dtype=BF16):
    return jnp.where(mask, 1.0, 0.0).astype(dtype)


def split(x):
    high = x.astype(BF16).astype(F32)
    return high, (x - high).astype(BF16).astype(F32)


def split3(x):
    high, mid = split(x)
    return high, mid, x - high - mid


def fetch(sources, targets, sems):
    copies = [pltpu.make_async_copy(a, b, sems.at[n]) for n, (a, b) in enumerate(zip(sources, targets))]
    for copy in copies:
        copy.start()
    return copies


def pack_kernel(
    hbm_rows, hbm_home, hbm_other, hbm_kind, hbm_image, hbm_pos, hbm_feat,
    send, lists,
    rows, home, other, kind, image, pos, feat, block, sems,
):
    copies = fetch(
        (hbm_rows, hbm_home, hbm_other, hbm_kind, hbm_image, hbm_pos, hbm_feat),
        (rows, home, other, kind, image, pos.at[0:3, :], feat),
        sems,
    )
    rep = lax.axis_index("rep")
    atoms = feat.shape[0]
    count = home.shape[1]
    pos[3:8, :] = jnp.zeros((5, atoms), F32)
    block[...] = jnp.zeros_like(block)
    for copy in copies:
        copy.wait()
    pick = ones_where(iota((atoms, TILE), 0) == rows[pl.ds(rep, 1), :])
    send[0:TILE, :] = dot(pick, feat[...], TN).astype(BF16)
    parts = jnp.concatenate([*split3(pos[...]), jnp.zeros_like(pos)], axis=0).astype(BF16)
    moved = dot(parts, pick).astype(BF16)
    send[TILE : TILE + SIDE, 0:TILE] = moved[0:SIDE]
    send[TILE : TILE + SIDE, TILE : 2 * TILE] = moved[SIDE : 2 * SIDE]
    for q in range(4):

        @pl.when(rep == q)
        def _(q=q):
            span = slice(q * count, (q + 1) * count)
            block[0:1, span] = home[...]
            block[1:2, span] = other[...]
            block[2:3, span] = kind[...]
            block[3:6, span] = image[...]

    for q in range(4):
        lists[8 * q : 8 * q + 8, :] = block[...]


def local_kernel(hbm_decay, pos, rates, places, terms, decay, wide, sems):
    [copy] = fetch([hbm_decay], [decay], sems)
    places[...] = jnp.zeros_like(places)
    wide[...] = jnp.zeros_like(wide)
    copy.wait()
    for k in range(rates.shape[0]):
        rates[k : k + 1, :] = jnp.full((1, rates.shape[1]), decay[k], F32)
    for t in range(2):
        places[t, 0:3, :] = pos[:, t * TILE : (t + 1) * TILE]
        at = [places[t][c : c + 1, :] for c in range(3)]
        row = iota((8, TILE), 0)
        factors = jnp.where(row == 0, at[0] * at[0] + at[1] * at[1] + at[2] * at[2], 0.0)
        factors = jnp.where(row == 1, 1.0, factors)
        for c in range(3):
            factors = jnp.where(row == 2 + c, at[c], factors)
        high, mid, low = split3(factors)
        for n, part in enumerate((high, mid, low, high, mid, high, mid, low)):
            wide[8 * n : 8 * n + 8, :] = part
        terms[t] = jnp.transpose(wide[...]).astype(BF16)[:, 0:DEPTH]


def plan_kernel(count, lists, rates, plan, reals):
    rep = lax.axis_index("rep")
    lanes = lists.shape[1]
    table = lists[0:8, :] + lists[8:16, :] + lists[16:24, :] + lists[24:32, :]
    home, other = table[0:1, :], table[1:2, :]
    valid = jnp.where(iota((1, lanes), 1) < 4 * count, 1, 0)
    ahead = ones_where(iota((lanes, lanes), 0) < iota((lanes, lanes), 1))

    def before(first, second):
        both = jnp.where(iota((16, lanes), 0) < 8, first, second)
        found = dot(both.astype(F32).astype(BF16), ahead).astype(I32)
        return found[0:1, :], found[8:9, :]

    def total(x):
        return jnp.sum(x.astype(F32), axis=1, keepdims=True).astype(I32)

    local = jnp.where(other < 2, valid, 0)
    start = jnp.zeros((1, 1), I32)
    quota = jnp.zeros((1, 1), I32)
    for q in range(4):
        room = jnp.maximum(count - total(jnp.where(other == 2 + q, valid, 0)), 0)
        start = start + jnp.where(q < rep, room, 0)
        quota = quota + jnp.where(q == rep, room, 0)
    turn, _ = before(local, local)
    taken = jnp.where(turn >= start, local, 0) * jnp.where(turn < start + quota, 1, 0)
    mine = taken + jnp.where(other == 2 + rep, valid, 0)
    first = jnp.where(home == 0, mine, 0)
    second = mine - first
    place_first, place_second = before(first, second)
    quads_first = (total(first) + (QUAD - 1)) // QUAD
    quads_second = (total(second) + (QUAD - 1)) // QUAD
    place = jnp.where(first > 0, place_first, place_second + quads_first * QUAD)
    place = jnp.where(mine > 0, place, -1)
    put = ones_where(iota((lanes, lanes), 0) == place)
    row = iota((8, lanes), 0)
    fields = jnp.where(row == 1, jnp.minimum(table, 2), table)
    fields = jnp.where(row == 6, 1, fields).astype(F32)
    rate = jnp.zeros((1, lanes), F32)
    for k in range(rates.shape[0]):
        rate = jnp.where(table[2:3, :] == k, rates[k : k + 1, :], rate)
    parts = split3(rate)
    rate = jnp.zeros((8, lanes), F32)
    for n in range(3):
        rate = jnp.where(row == n, parts[n], rate)
    fields = jnp.concatenate([fields, rate], axis=0).astype(BF16)
    listed = dot(fields, put, NT)
    counts = listed[0:8, :].astype(I32)
    plan[...] = jnp.where(row == 7, quads_first + quads_second, counts)
    rate = listed[8:9, :] + listed[9:10, :] + listed[10:11, :]
    empty = 1.0 - listed[6:7, :]
    reals[...] = jnp.where(row == 0, rate + empty, jnp.where(row == 7, empty * FAR, listed[0:8, :] * EDGE))


def halo_places(halo):
    side = halo[TILE : TILE + SIDE, :].astype(F32)
    return side[0:8, 0:TILE] + side[8:16, 0:TILE] + side[0:8, TILE : 2 * TILE]


def pair_fields(plan, reals, p):
    return plan[1, p], plan[2, p], reals[0, p], [reals[3 + c, p] for c in range(3)], reals[7, p]


def exponent(terms, places, slot, rate, shift, away):
    at = [places[slot][c : c + 1, :] + shift[c] for c in range(3)]
    at[0] = at[0] + away
    row = iota((8, TILE), 0)
    square = at[0] * at[0] + at[1] * at[1] + at[2] * at[2]
    factors = jnp.where(row == 0, -rate, jnp.where(row == 1, -rate * square, 0.0))
    for c in range(3):
        factors = jnp.where(row == 2 + c, at[c] * (2.0 * rate), factors)
    high, mid, low = split3(factors)
    across = jnp.concatenate([high, high, high, mid, mid, low, low, mid], axis=0).astype(BF16)
    return dot(terms, across)


def halo_kernel(halo, home_places, radial, feat, mapped, places):
    atoms = feat.shape[0]
    places[0:2] = home_places[...]
    places[2] = halo_places(halo)
    for k in range(radial.shape[0]):
        mapped[k, 0:atoms, :] = dot(feat[...], radial[k]).astype(BF16)
        mapped[k, atoms : atoms + TILE, :] = dot(halo[0:TILE, :], radial[k]).astype(BF16)


def forward_kernel(hbm_plan, hbm_reals, terms, mapped, places, partial, plan, reals, message, held, sems):
    copies = fetch((hbm_plan, hbm_reals), (plan, reals), sems)
    atoms = 2 * TILE
    message[...] = jnp.zeros_like(message)
    for copy in copies:
        copy.wait()

    held[...] = jnp.zeros_like(held)
    steps = plan[7, 0]

    def step(q, carry):
        now, ago = jnp.minimum(q, steps - 1) * QUAD, jnp.maximum(q - 1, 0) * QUAD
        home = plan[0, now]
        fields = [pair_fields(plan, reals, now + u) for u in range(QUAD)]
        powers = [exponent(terms[home], places, f[0], *f[2:]) for f in fields]
        across = [mapped[plan[2, ago + u], tile_of(plan[1, ago + u]), :] for u in range(QUAD)]
        message[plan[0, ago]] += dot(held[...], jnp.concatenate(across, axis=0))
        for u in range(QUAD):
            held[:, u * TILE : (u + 1) * TILE] = jnp.exp(powers[u]).astype(BF16)
        return carry

    lax.fori_loop(0, jnp.where(steps > 0, steps + 1, 0), step, 0)
    for t in range(2):
        low = message[t].astype(BF16)
        for q in range(4):
            partial[q * atoms + t * TILE : q * atoms + (t + 1) * TILE, :] = low


def tile_of(slot):
    return pl.ds(pl.multiple_of(slot * TILE, TILE), TILE)


def marks(*which):
    row = iota((SIDE, TILE), 0)
    found = jnp.zeros((SIDE, TILE), F32)
    for r in which:
        found = jnp.where(row == r, 1.0, found)
    return found


def tile_sums(found, block, side):
    found = found[0:SIDE] + found[SIDE : 2 * SIDE]
    at = [block[c : c + 1, :] for c in range(3)]
    zeroth = found[0:1, :]
    once = [found[1 + c : 2 + c, :] for c in range(3)]
    side[...] = jnp.zeros_like(side)
    for c in range(3):
        side[c : c + 1, :] = once[c] - at[c] * zeroth
    for n, (a, b) in enumerate(COMPONENT_PAIRS):
        at_row = 4 + n if n < 3 else 5 + n
        twice = found[at_row : at_row + 1, :]
        side[8 + n : 9 + n, :] = -0.5 * (twice - at[b] * once[a] - at[a] * once[b] + at[a] * at[b] * zeroth)


def atom_kernel(partial, mixing, readout, adjoint, flipped, mixing_part):
    rep = lax.axis_index("rep")
    channels = mixing.shape[0]
    atoms = 2 * TILE
    message = partial[0:atoms, :].astype(F32)
    for q in range(1, 4):
        message = message + partial[q * atoms : (q + 1) * atoms, :].astype(F32)
    packed = message.astype(BF16)
    mixed = dot(packed, mixing[...])
    gate = jax.nn.sigmoid(mixed)
    slope = (readout[...] * gate * (1.0 + mixed * (1.0 - gate))).astype(BF16)
    adjoint[...] = dot(slope, mixing[...], NT).astype(BF16).reshape(2, TILE, channels)
    for t in range(2):
        flipped[t] = dot(mixing[...], slope[t * TILE : (t + 1) * TILE, :], NT).astype(BF16)
    half = channels // 2
    share = channels // 4
    gradient = None
    for odd in range(2):
        take_rows = ones_where(iota((half, channels), 1) == 2 * iota((half, channels), 0) + odd)
        lane = iota((channels, TILE), 1) - odd * share
        inside = jnp.where(lane >= 0, 1, 0) * jnp.where(lane < share, 1, 0)
        take_cols = ones_where(jnp.where(inside > 0, lane + rep * share, -1) == iota((channels, TILE), 0))
        left = dot(take_rows, packed, NT).astype(BF16)
        right = dot(slope, take_cols).astype(BF16)
        part = dot(left, right)
        gradient = part if gradient is None else gradient + part
    mixing_part[...] = gradient


def backward_kernel(
    hbm_plan, hbm_reals, adjoint, flipped, places, terms, radial, mapped,
    back, home_grads, home_sums,
    plan, reals, spread, grads, bases, sums, side, held, weights, sems,
):
    copies = fetch((hbm_plan, hbm_reals), (plan, reals), sems)
    kinds = radial.shape[0]
    for t in range(2):
        for k in range(kinds):
            spread[t * kinds + k] = dot(radial[k], flipped[t]).astype(BF16)

    left_marks = (marks(1, 4, 8, 9), marks(2, 5, 10), marks(3, 6))
    right_marks = (marks(4), marks(5, 8), marks(6, 9, 10))
    left_one, right_one = marks(0), marks(0, 1, 2, 3)
    for t in range(SLOTS):
        block = places[t]
        left, right = left_one, right_one
        for c in range(3):
            left = left + left_marks[c] * block[c : c + 1, :]
            right = right + right_marks[c] * block[c : c + 1, :]
        bases[t, 0:SIDE, :] = left
        bases[t, SIDE : 2 * SIDE, :] = right
    sums[...] = jnp.zeros_like(sums)
    grads[...] = jnp.zeros_like(grads)
    for copy in copies:
        copy.wait()

    def monomials(t, left_shift, right_shift):
        base = bases[t]
        high, low = split((base[0:SIDE] + left_shift) * (base[SIDE : 2 * SIDE] + right_shift))
        both = jnp.concatenate([high, low], axis=0).astype(BF16)
        return jnp.concatenate([both, both], axis=1)

    held[...] = jnp.zeros_like(held)
    weights[...] = jnp.zeros_like(weights)
    steps = plan[7, 0]

    def step(q, carry):
        now, ago = jnp.minimum(q, steps - 1) * QUAD, jnp.maximum(q - 1, 0) * QUAD
        home, home_ago = plan[0, now], plan[0, ago]
        home_sum = None
        for u in range(QUAD):
            slot, kind, rate, shift, away = pair_fields(plan, reals, now + u)
            power = exponent(terms[home], places, slot, rate, shift, away)
            pull = dot(adjoint[home], mapped[kind, tile_of(slot), :], NT)

            slot, kind, _, shift, _ = pair_fields(plan, reals, ago + u)
            left_shift = sum(left_marks[c] * shift[c] for c in range(3))
            right_shift = sum(right_marks[c] * shift[c] for c in range(3))
            far = monomials(slot, left_shift, right_shift)
            near = monomials(home_ago, -left_shift, -right_shift)
            high, low = weights[u, 0], weights[u, 1]
            part = dot(far, jnp.concatenate([high, low], axis=1), NT)
            home_sum = part if home_sum is None else home_sum + part
            sums[slot] += dot(near, jnp.concatenate([high, low], axis=0))
            grads[slot] += dot(spread[home_ago * kinds + kind], held[u])

            kernel = jnp.exp(power)
            held[u] = kernel.astype(BF16)
            weight = (kernel * (-2.0 * rate)) * pull
            high = weight.astype(BF16)
            weights[u, 0] = high
            weights[u, 1] = (weight - high.astype(F32)).astype(BF16)
        sums[home_ago] += home_sum
        return carry

    lax.fori_loop(0, jnp.where(steps > 0, steps + 1, 0), step, 0)
    back[0:TILE, :] = jnp.transpose(grads[2]).astype(BF16)
    tile_sums(sums[2], places[2], side)
    high, low = split(side[...])
    back[TILE : TILE + SIDE, 0:TILE] = high.astype(BF16)
    back[TILE : TILE + SIDE, TILE : 2 * TILE] = low.astype(BF16)
    home_grads[...] = grads[0:2]
    home_sums[...] = sums[0:2]


def own_kernel(home_grads, home_sums, places, own_grad, own_side, side):
    for t in range(2):
        own_grad[t * TILE : (t + 1) * TILE, :] = jnp.transpose(home_grads[t])
        tile_sums(home_sums[t], places[t], side)
        own_side[:, t * TILE : (t + 1) * TILE] = side[...]


def return_kernel(rows, got, own_grad, own_side, payload):
    rep = lax.axis_index("rep")
    atoms = own_grad.shape[0]
    pick = ones_where(iota((atoms, TILE), 0) == rows[pl.ds(rep, 1), :])
    grad = (own_grad[...] + dot(pick, got[0:TILE, :])).astype(BF16)
    came = got[TILE : TILE + SIDE, :]
    side = own_side[...] + dot(came[:, 0:TILE], pick, NT) + dot(came[:, TILE : 2 * TILE], pick, NT)
    high, low = split(side)
    both = jnp.concatenate([high, low], axis=0).astype(BF16)
    height = atoms + 2 * SIDE
    for q in range(4):
        payload[q * height : q * height + atoms, :] = grad
        payload[q * height + atoms : (q + 1) * height, :] = both


def final_kernel(payload, grad, forces, virials):
    atoms = grad.shape[0]
    height = atoms + 2 * SIDE
    total = None
    side = None
    for q in range(4):
        part = payload[q * height : q * height + atoms, :].astype(F32)
        total = part if total is None else total + part
        both = payload[q * height + atoms : (q + 1) * height, :].astype(F32)
        part = both[0:SIDE] + both[SIDE : 2 * SIDE]
        side = part if side is None else side + part
    grad[...] = total.astype(BF16)
    forces[...] = side[0:3]
    virials[...] = side[8:14]


def mixing_kernel(mixing_parts, grad_mixing):
    found = jnp.sum(mixing_parts[...], axis=0, keepdims=True)
    share = grad_mixing.shape[1]
    grad_mixing[0:1, :] = found[:, 0:share]
    grad_mixing[1:2, :] = found[:, share : 2 * share]


def call(kernel, outs, ins, scratch=(), hbm=0, sems=0, away=(), flops=0, moved=1 << 20, limit=32 << 20):
    vmem = pl.BlockSpec(memory_space=pltpu.VMEM)
    stay = pl.BlockSpec(memory_space=pl.ANY)
    return pl.pallas_call(
        kernel,
        out_shape=[jax.ShapeDtypeStruct(shape, dtype) for shape, dtype in outs],
        in_specs=[stay if n < hbm or n in away else vmem for n in range(len(ins))],
        out_specs=[vmem] * len(outs),
        scratch_shapes=list(scratch) + ([pltpu.SemaphoreType.DMA((sems,))] if sems else []),
        compiler_params=pltpu.CompilerParams(vmem_limit_bytes=limit),
        cost_estimate=pl.CostEstimate(flops=flops, bytes_accessed=moved, transcendentals=0),
    )(*ins)


def on_device(
    features, positions, radial, mixing, readout, decay,
    send_rows, pair_home, pair_other, pair_kind, pair_image,
):
    atoms, channels = features.shape
    kinds = radial.shape[0]
    count = pair_home.shape[0]
    doms, reps = lax.axis_size("dom"), lax.axis_size("rep")
    lanes = 2 * TILE
    height = atoms + 2 * SIDE
    assert reps == len(OFFSETS) and atoms == 2 * TILE and 4 * count <= lanes - 4 * QUAD
    assert channels == 2 * doms

    def hop(array, sign):
        ways = [
            (d * reps + r, (d + sign * OFFSETS[r]) % doms * reps + r)
            for d in range(doms)
            for r in range(reps)
        ]
        return lax.ppermute(array, ("dom", "rep"), ways)

    def swap(array, axis):
        return lax.all_to_all(array, axis, 0, 0, tiled=True)

    vmem, smem = pltpu.VMEM, pltpu.SMEM
    sent = [send_rows, *(x.reshape(1, count) for x in (pair_home, pair_other, pair_kind))]
    sent += [pair_image, positions, features]
    send, lists = call(
        pack_kernel,
        [((TILE + SIDE, channels), BF16), ((32, lanes), I32)],
        sent,
        [vmem(x.shape, x.dtype) for x in sent[:5]]
        + [vmem((8, atoms), F32), vmem(features.shape, BF16), vmem((8, lanes), I32)],
        hbm=len(sent),
        sems=len(sent),
        flops=1 << 30,
        limit=63 << 20,
    )
    halo = hop(send, 1)
    lists = swap(lists, "rep")
    rates, home_places, terms = call(
        local_kernel,
        [((kinds, lanes), F32), ((2, 8, TILE), F32), ((2, TILE, DEPTH), BF16)],
        [decay, positions],
        [smem(decay.shape, F32), vmem((TILE, TILE), F32)],
        hbm=1,
        sems=1,
        flops=1 << 32,
    )
    plan, reals = call(
        functools.partial(plan_kernel, count),
        [((8, lanes), I32), ((8, lanes), F32)],
        [lists, rates],
        flops=1 << 20,
    )
    tables = [smem((8, lanes), I32), smem((8, lanes), F32)]
    mapped, places = call(
        halo_kernel,
        [((kinds, SLOTS * TILE, channels), BF16), ((SLOTS, 8, TILE), F32)],
        [halo, home_places, radial, features],
        flops=1 << 30,
    )
    [partial] = call(
        forward_kernel,
        [((reps * atoms, channels), BF16)],
        [plan, reals, terms, mapped, places],
        tables + [vmem((2, TILE, channels), F32), vmem((TILE, QUAD * TILE), BF16)],
        hbm=2,
        sems=2,
        flops=1 << 31,
    )
    partial = swap(partial, "rep")
    adjoint, flipped, mixing_part = call(
        atom_kernel,
        [((2, TILE, channels), BF16), ((2, channels, TILE), BF16), ((channels // 2, TILE), F32)],
        [partial, mixing, readout.reshape(1, channels)],
        flops=1 << 28,
    )
    mixing_parts = swap(mixing_part, "dom")
    back, home_grads, home_sums = call(
        backward_kernel,
        [((TILE + SIDE, channels), BF16), ((2, channels, TILE), F32), ((2, 2 * SIDE, TILE), F32)],
        [plan, reals, adjoint, flipped, places, terms, radial, mapped],
        tables
        + [
            vmem((2 * kinds, channels, TILE), BF16),
            vmem((SLOTS, channels, TILE), F32),
            vmem((SLOTS, 2 * SIDE, TILE), F32),
            vmem((SLOTS, 2 * SIDE, TILE), F32),
            vmem((SIDE, TILE), F32),
            vmem((QUAD, TILE, TILE), BF16),
            vmem((QUAD, 2, TILE, TILE), BF16),
        ],
        hbm=2,
        sems=2,
        flops=1 << 33,
    )
    got = hop(back, -1)
    own_grad, own_side = call(
        own_kernel,
        [((atoms, channels), F32), ((SIDE, atoms), F32)],
        [home_grads, home_sums, places],
        [vmem((SIDE, TILE), F32)],
        flops=1 << 30,
    )
    [payload] = call(
        return_kernel,
        [((reps * height, channels), BF16)],
        [send_rows, got, own_grad, own_side],
        flops=1 << 24,
    )
    payload = swap(payload, "rep")
    [grad_mixing] = call(mixing_kernel, [((2, channels // reps), F32)], [mixing_parts])
    grad, forces, virials = call(
        final_kernel,
        [((atoms, channels), BF16), ((3, atoms), F32), ((6, atoms), F32)],
        [payload],
    )
    return grad, forces, virials, grad_mixing


def solution(mesh):
    in_specs = (
        P("dom", None),
        P(None, "dom"),
        P(),
        P(),
        P(),
        P(),
        P(None, "dom"),
        P(("dom", "rep")),
        P(("dom", "rep")),
        P(("dom", "rep")),
        P(None, ("dom", "rep")),
    )
    out_specs = (P("dom", None), P(None, "dom"), P(None, "dom"), P("dom", "rep"))
    return jax.shard_map(
        on_device, mesh=mesh, in_specs=in_specs, out_specs=out_specs, check_vma=False
    )
```

time: 98.7 us -> 84.4 us (0.86)
  blocking collectives: 39.1 us -> 18.3 us
  starting transfers between devices: 19.4 us -> 31.3 us
  local copies, waits for them, and re-layouts: 7.73 us -> 0.03 us
  waiting for transfers between devices: 11.8 us -> 14.3 us
  Pallas kernels: 19.4 us -> 18.3 us
    all_to_all x3 -> x1, blocking collectives: 39.1 us -> 18.3 us  [swap(): return lax.all_to_all(array, axis, 0, 0, tiled=True)]
    all_to_all x1 -> x3, starting transfers between devices: 12.1 us -> 24.4 us  [swap(): return lax.all_to_all(array, axis, 0, 0, tiled=True)]
    unnamed x32 -> x14, local copies, waits for them, and re-layouts: 7.73 us -> 0.03 us
    ppermute x2, waiting for transfers between devices: 3.23 us -> 5.86 us  [hop(): return lax.ppermute(array, ('dom', 'rep'), ways)]
    pallas_call x6 -> x11, Pallas kernels: 19.4 us -> 18.3 us  [call(): pl.pallas_call(kernel, out_shape=[jax.ShapeDtypeStruct(shape, dtype) for...]
    all_to_all x1 -> x3, waiting for transfers between devices: 8.58 us -> 8.46 us  [swap(): return lax.all_to_all(array, axis, 0, 0, tiled=True)]
  transfers between devices with their start and end apart: 3 -> 5, of which waited for: 2 -> 4; matrix products, arithmetic and copies ran while one was open for 0% -> 0% of each run, Pallas kernels for 1% -> 12%
where the time goes in v2:
time: 84.4 us; the launch traced here: 82.9 us
  starting transfers between devices  31.3 us (37%)
  Pallas kernels  18.3 us (22%)
  blocking collectives  18.3 us (22%)
  waiting for transfers between devices  14.3 us (17%)
    all_to_all x3, starting transfers between devices, swap(): return lax.all_to_all(array, axis, 0, 0, tiled=True)  24.4 us
    pallas_call x11, Pallas kernels, call(): pl.pallas_call(kernel, out_shape=[jax.ShapeDtypeStruct(shape, dtype) for...  18.3 us
    all_to_all x1, blocking collectives, swap(): return lax.all_to_all(array, axis, 0, 0, tiled=True)  18.3 us
    all_to_all x3, waiting for transfers between devices, swap(): return lax.all_to_all(array, axis, 0, 0, tiled=True)  8.46 us
    ppermute x2, starting transfers between devices, hop(): return lax.ppermute(array, ('dom', 'rep'), ways)  6.89 us
    ppermute x2, waiting for transfers between devices, hop(): return lax.ppermute(array, ('dom', 'rep'), ways)  5.86 us
  transfers between devices with their start and end apart: 5, of which 4 were waited for; matrix products, arithmetic and copies ran while one was open for 0% of the time, Pallas kernels for 12%

profile of v2, /device:TPU:1, one launch (start us, length us, event | category | flops | bytes accessed | tf_op | source)
XLA Modules:
  0.0 82.9 jit_solution(12798386812518839116)
XLA Ops:
  0.6 0.0 copy-start.4
  0.6 0.0 copy-start.6
  0.7 1.9 %shard_map.138 = (bf16[144,256]{1,0:T(8,128)(2,1)}, s32[32,256]{1,0:T(8,128)}) custom-call(s32[4,128]{1,0:T(4,128)} %rows.1, s32[1,48]{1,0:T(1,128)} %bitcast.21, s32[1,48]{1,0:T(1,128)} %bitcast.22, s32[1,48]{1,0:T(1,128)} %bitcast.23, s32[3,48]{1,0:T(4,128)} %hbm_image.1, f32[3,256]{1,0:T(4,128)} %pos.1, bf16[256,256]{1,0:T(8,128)(2,1)} %feat.1), custom_call_target="tpu_custom_call" | custom-call | flops 1073741824 | bytes 1048576 | tf_op jit(solution)/shard_map/pallas_call | solution.py:404
  2.6 5.1 %all-to-all-start = ((s32[4,8,256]{2,1,0:T(8,128)}), s32[4,8,256]{2,1,0:T(8,128)S(1)}, u32[]{:S(2)}, u32[]{:S(2)}) async-start(s32[4,8,256]{2,1,0:T(8,128)} %bitcast.20), calls=%async_computation | async-start | bytes 65536 | tf_op jit(solution)/shard_map/all_to_all | solution.py:437
  7.7 0.0 copy-start.1
  7.7 0.0 copy-start.2
  7.7 4.1 %collective-permute-start = (bf16[144,256]{1,0:T(8,128)(2,1)}, bf16[144,256]{1,0:T(8,128)(2,1)S(1)}, u32[]{:S(2)}, u32[]{:S(2)}) collective-permute-start(bf16[144,256]{1,0:T(8,128)(2,1)} %get-tuple-element.29), channel_id=1, source_target_pairs={{0,4},{1,509},{2,10},{3,507},{4,8},{5,1},{6,14},{7,511},{8,12},{9,... | collective-permute-start | bytes 221192 | tf_op jit(solution)/shard_map/ppermute | solution.py:434
  11.8 0.0 copy-done.4
  11.8 0.0 copy-done.6
  11.8 0.7 shard_map.139
  12.5 0.0 all-to-all-done
  12.5 0.5 shard_map.140
  12.9 2.8 %collective-permute-done.halo = bf16[144,256]{1,0:T(8,128)(2,1)S(1)} collective-permute-done((bf16[144,256]{1,0:T(8,128)(2,1)}, bf16[144,256]{1,0:T(8,128)(2,1)S(1)}, u32[]{:S(2)}, u32[]{:S(2)}) %collective-permute-start) | collective-permute-done | bytes 73760 | tf_op jit(solution)/shard_map/ppermute | solution.py:434
  15.8 0.0 copy-done.1
  15.8 0.0 copy-done.2
  15.8 0.6 shard_map.141
  16.4 0.0 copy-start.3
  16.4 0.0 copy-start.5
  16.4 3.6 %shard_map.142 = bf16[1024,256]{1,0:T(8,128)(2,1)S(1)} custom-call(s32[8,256]{1,0:T(8,128)S(1)} %get-tuple-element.26.hbm_plan, f32[8,256]{1,0:T(8,128)S(1)} %get-tuple-element.27.hbm_reals, bf16[2,128,64]{2,1,0:T(8,128)(2,1)S(1)} %get-tuple-element.28.terms, bf16[8,384,256]{2,1,0:T(8,128)(2,1)S(1)} %get-tuple-element.31.mapped, ...), custom_call_target="tpu_custom_call" | custom-call | flops 2147483648 | bytes 1048576 | tf_op jit(solution)/shard_map/pallas_call | solution.py:404
  20.0 18.3 %all_to_all.44 = bf16[4,256,256]{2,1,0:T(8,128)(2,1)S(1)} all-to-all(bf16[4,256,256]{2,1,0:T(8,128)(2,1)S(1)} %bitcast.16), channel_id=1, replica_groups=mesh['dom'=128,'rep'=4] {'rep'}, dimensions={0} | all-to-all | bytes 1048576 | tf_op jit(solution)/shard_map/all_to_all | solution.py:437
  38.3 0.0 copy-done.3
  38.3 0.0 copy-done.5
  38.3 1.3 %shard_map.143 = (bf16[2,128,256]{2,1,0:T(8,128)(2,1)S(1)}, bf16[2,256,128]{2,1,0:T(8,128)(2,1)S(1)}, f32[128,128]{1,0:T(8,128)}) custom-call(bf16[1024,256]{1,0:T(8,128)(2,1)S(1)} %bitcast.15, bf16[256,256]{1,0:T(8,128)(2,1)S(1)} %copy-done.3, f32[1,256]{1,0:T(1,128)S(1)} %bitcast.19), custom_call_target="tpu_custom_call" | custom-call | flops 268435456 | bytes 1048576 | tf_op jit(solution)/shard_map/pallas_call | solution.py:404
  39.6 14.3 %all-to-all-start.3 = ((f32[128,1,128]{2,1,0:T(1,128)}), f32[128,1,128]{2,1,0:T(1,128)S(1)}, u32[]{:S(2)}, u32[]{:S(2)}) async-start(f32[128,1,128]{2,1,0:T(1,128)} %bitcast.11), calls=%async_computation.3 | async-start | bytes 131072 | tf_op jit(solution)/shard_map/all_to_all | solution.py:437
  53.9 7.1 %shard_map.144 = (bf16[144,256]{1,0:T(8,128)(2,1)S(1)}, f32[2,256,128]{2,1,0:T(8,128)S(1)}, f32[2,32,128]{2,1,0:T(8,128)S(1)}) custom-call(s32[8,256]{1,0:T(8,128)S(1)} %get-tuple-element.26.hbm_plan, f32[8,256]{1,0:T(8,128)S(1)} %get-tuple-element.27.hbm_reals, bf16[2,128,256]{2,1,0:T(8,128)(2,1)S(1)} %get-tuple-element.33.adjoint, ...), custom_call_target="tpu_custom_call" | custom-call | flops 8589934592 | bytes 1048576 | tf_op jit(solution)/shard_map/pallas_call | solution.py:404
  61.1 2.8 %collective-permute-start.1 = (bf16[144,256]{1,0:T(8,128)(2,1)S(1)}, bf16[144,256]{1,0:T(8,128)(2,1)S(1)}, u32[]{:S(2)}, u32[]{:S(2)}) collective-permute-start(bf16[144,256]{1,0:T(8,128)(2,1)S(1)} %get-tuple-element.35), channel_id=1, source_target_pairs={{0,508},{1,5},{2,506},{3,11},{4,0},{5,9},{6,510},{7,15},{8,4},{9,1... | collective-permute-start | bytes 221192 | tf_op jit(solution)/shard_map/ppermute | solution.py:434
  63.9 0.0 copy-start
  63.9 0.1 shard_map.145
  64.0 3.0 %collective-permute-done.1.got = bf16[144,256]{1,0:T(8,128)(2,1)S(1)} collective-permute-done((bf16[144,256]{1,0:T(8,128)(2,1)S(1)}, bf16[144,256]{1,0:T(8,128)(2,1)S(1)}, u32[]{:S(2)}, u32[]{:S(2)}) %collective-permute-start.1) | collective-permute-done | bytes 73760 | tf_op jit(solution)/shard_map/ppermute | solution.py:434
  67.1 0.0 copy-done
  67.1 1.0 %shard_map.146 = bf16[1152,256]{1,0:T(8,128)(2,1)} custom-call(s32[4,128]{1,0:T(4,128)S(1)} %copy-done, bf16[144,256]{1,0:T(8,128)(2,1)S(1)} %collective-permute-done.1.got, f32[256,256]{1,0:T(8,128)S(1)} %get-tuple-element.38.own_grad, f32[16,256]{1,0:T(8,128)S(1)} %get-tuple-element.39.own_side), custom_call_target="tpu_custom_call" | custom-call | flops 16777216 | bytes 1048576 | tf_op jit(solution)/shard_map/pallas_call | solution.py:404
  68.1 0.7 all-to-all-done.3
  68.8 5.0 %all-to-all-start.2 = ((bf16[4,288,256]{2,1,0:T(8,128)(2,1)}), bf16[4,288,256]{2,1,0:T(8,128)(2,1)S(1)}, u32[]{:S(2)}, u32[]{:S(2)}) async-start(bf16[4,288,256]{2,1,0:T(8,128)(2,1)} %bitcast.8), calls=%async_computation.2 | async-start | bytes 1179648 | tf_op jit(solution)/shard_map/all_to_all | solution.py:437
  73.8 0.7 shard_map.148
  74.4 7.8 %all-to-all-done.2 = bf16[4,288,256]{2,1,0:T(8,128)(2,1)S(1)} async-done(((bf16[4,288,256]{2,1,0:T(8,128)(2,1)}), bf16[4,288,256]{2,1,0:T(8,128)(2,1)S(1)}, u32[]{:S(2)}, u32[]{:S(2)}) %all-to-all-start.2) | async-done | bytes 589856 | tf_op jit(solution)/shard_map/all_to_all | solution.py:437
  82.2 0.7 shard_map.147
Async XLA Ops:
  0.6 11.1 %copy-start.4 = (f32[3,256]{1,0:T(4,128)S(1)}, f32[3,256]{1,0:T(4,128)}, u32[]{:S(2)}) copy-start(f32[3,256]{1,0:T(4,128)} %pos.1) | copy-start | bytes 9220
  0.6 11.1 %copy-start.6 = (f32[8]{0:T(128)S(1)}, f32[8]{0:T(128)}, u32[]{:S(2)}) copy-start(f32[8]{0:T(128)} %hbm_decay.1) | copy-start | bytes 100
  2.6 9.9 %all-to-all-start = ((s32[4,8,256]{2,1,0:T(8,128)}), s32[4,8,256]{2,1,0:T(8,128)S(1)}, u32[]{:S(2)}, u32[]{:S(2)}) async-start(s32[4,8,256]{2,1,0:T(8,128)} %bitcast.20), calls=%async_computation | async-start | bytes 65536 | tf_op jit(solution)/shard_map/all_to_all | solution.py:437
  7.7 8.1 %copy-start.1 = (bf16[8,256,256]{2,1,0:T(8,128)(2,1)S(1)}, bf16[8,256,256]{2,1,0:T(8,128)(2,1)}, u32[]{:S(2)}) copy-start(bf16[8,256,256]{2,1,0:T(8,128)(2,1)} %radial.3) | copy-start | bytes 3145732
  7.7 8.1 %copy-start.2 = (bf16[256,256]{1,0:T(8,128)(2,1)S(1)}, bf16[256,256]{1,0:T(8,128)(2,1)}, u32[]{:S(2)}) copy-start(bf16[256,256]{1,0:T(8,128)(2,1)} %feat.1) | copy-start | bytes 393220
  7.7 8.1 %collective-permute-start = (bf16[144,256]{1,0:T(8,128)(2,1)}, bf16[144,256]{1,0:T(8,128)(2,1)S(1)}, u32[]{:S(2)}, u32[]{:S(2)}) collective-permute-start(bf16[144,256]{1,0:T(8,128)(2,1)} %get-tuple-element.29), channel_id=1, source_target_pairs={{0,4},{1,509},{2,10},{3,507},{4,8},{5,1},{6,14},{7,511},{8,12},{9,... | collective-permute-start | bytes 221192 | tf_op jit(solution)/shard_map/ppermute | solution.py:434
  16.4 21.9 %copy-start.3 = (bf16[256,256]{1,0:T(8,128)(2,1)S(1)}, bf16[256,256]{1,0:T(8,128)(2,1)}, u32[]{:S(2)}) copy-start(bf16[256,256]{1,0:T(8,128)(2,1)} %mixing.1) | copy-start | bytes 393220
  16.4 21.9 %copy-start.5 = (f32[256]{0:T(256)S(1)}, f32[256]{0:T(256)}, u32[]{:S(2)}) copy-start(f32[256]{0:T(256)} %param.15) | copy-start | bytes 3076
  39.6 29.1 %all-to-all-start.3 = ((f32[128,1,128]{2,1,0:T(1,128)}), f32[128,1,128]{2,1,0:T(1,128)S(1)}, u32[]{:S(2)}, u32[]{:S(2)}) async-start(f32[128,1,128]{2,1,0:T(1,128)} %bitcast.11), calls=%async_computation.3 | async-start | bytes 131072 | tf_op jit(solution)/shard_map/all_to_all | solution.py:437
  61.1 6.0 %collective-permute-start.1 = (bf16[144,256]{1,0:T(8,128)(2,1)S(1)}, bf16[144,256]{1,0:T(8,128)(2,1)S(1)}, u32[]{:S(2)}, u32[]{:S(2)}) collective-permute-start(bf16[144,256]{1,0:T(8,128)(2,1)S(1)} %get-tuple-element.35), channel_id=1, source_target_pairs={{0,508},{1,5},{2,506},{3,11},{4,0},{5,9},{6,510},{7,15},{8,4},{9,1... | collective-permute-start | bytes 221192 | tf_op jit(solution)/shard_map/ppermute | solution.py:434
  63.9 3.2 %copy-start = (s32[4,128]{1,0:T(4,128)S(1)}, s32[4,128]{1,0:T(4,128)}, u32[]{:S(2)}) copy-start(s32[4,128]{1,0:T(4,128)} %rows.1) | copy-start | bytes 6148
  68.8 13.5 %all-to-all-start.2 = ((bf16[4,288,256]{2,1,0:T(8,128)(2,1)}), bf16[4,288,256]{2,1,0:T(8,128)(2,1)S(1)}, u32[]{:S(2)}, u32[]{:S(2)}) async-start(bf16[4,288,256]{2,1,0:T(8,128)(2,1)} %bitcast.8), calls=%async_computation.2 | async-start | bytes 1179648 | tf_op jit(solution)/shard_map/all_to_all | solution.py:437

commit v3 on v2

--- a/solution.py
+++ b/solution.py
@@ -98,16 +98,7 @@
         rates[k : k + 1, :] = jnp.full((1, rates.shape[1]), decay[k], F32)
     for t in range(2):
         places[t, 0:3, :] = pos[:, t * TILE : (t + 1) * TILE]
-        at = [places[t][c : c + 1, :] for c in range(3)]
-        row = iota((8, TILE), 0)
-        factors = jnp.where(row == 0, at[0] * at[0] + at[1] * at[1] + at[2] * at[2], 0.0)
-        factors = jnp.where(row == 1, 1.0, factors)
-        for c in range(3):
-            factors = jnp.where(row == 2 + c, at[c], factors)
-        high, mid, low = split3(factors)
-        for n, part in enumerate((high, mid, low, high, mid, high, mid, low)):
-            wide[8 * n : 8 * n + 8, :] = part
-        terms[t] = jnp.transpose(wide[...]).astype(BF16)[:, 0:DEPTH]
+        terms[t] = tile_terms(places[t], wide)
 
 
 def plan_kernel(count, lists, rates, plan, reals):
@@ -172,8 +163,8 @@
     return plan[1, p], plan[2, p], reals[0, p], [reals[3 + c, p] for c in range(3)], reals[7, p]
 
 
-def exponent(terms, places, slot, rate, shift, away):
-    at = [places[slot][c : c + 1, :] + shift[c] for c in range(3)]
+def exponent_factors(block, rate, shift, away):
+    at = [block[c : c + 1, :] + shift[c] for c in range(3)]
     at[0] = at[0] + away
     row = iota((8, TILE), 0)
     square = at[0] * at[0] + at[1] * at[1] + at[2] * at[2]
@@ -181,41 +172,69 @@
     for c in range(3):
         factors = jnp.where(row == 2 + c, at[c] * (2.0 * rate), factors)
     high, mid, low = split3(factors)
-    across = jnp.concatenate([high, high, high, mid, mid, low, low, mid], axis=0).astype(BF16)
-    return dot(terms, across)
-
-
-def halo_kernel(halo, home_places, radial, feat, mapped, places):
+    return jnp.concatenate([high, high, high, mid, mid, low, low, mid], axis=0).astype(BF16)
+
+
+def tile_terms(block, wide):
+    at = [block[c : c + 1, :] for c in range(3)]
+    row = iota((8, TILE), 0)
+    factors = jnp.where(row == 0, at[0] * at[0] + at[1] * at[1] + at[2] * at[2], 0.0)
+    factors = jnp.where(row == 1, 1.0, factors)
+    for c in range(3):
+        factors = jnp.where(row == 2 + c, at[c], factors)
+    high, mid, low = split3(factors)
+    for n, part in enumerate((high, mid, low, high, mid, high, mid, low)):
+        wide[8 * n : 8 * n + 8, :] = part
+    return jnp.transpose(wide[...]).astype(BF16)[:, 0:DEPTH]
+
+
+def forward_kernel(
+    hbm_plan, hbm_reals, halo, home_places, home_terms, radial, feat,
+    mapped, places, terms, partial,
+    plan, reals, wide, message, held, sems,
+):
+    copies = fetch((hbm_plan, hbm_reals), (plan, reals), sems)
     atoms = feat.shape[0]
     places[0:2] = home_places[...]
     places[2] = halo_places(halo)
+    terms[0:2] = home_terms[...]
+    wide[...] = jnp.zeros_like(wide)
+    terms[2] = tile_terms(places[2], wide)
     for k in range(radial.shape[0]):
         mapped[k, 0:atoms, :] = dot(feat[...], radial[k]).astype(BF16)
         mapped[k, atoms : atoms + TILE, :] = dot(halo[0:TILE, :], radial[k]).astype(BF16)
-
-
-def forward_kernel(hbm_plan, hbm_reals, terms, mapped, places, partial, plan, reals, message, held, sems):
-    copies = fetch((hbm_plan, hbm_reals), (plan, reals), sems)
-    atoms = 2 * TILE
     message[...] = jnp.zeros_like(message)
     for copy in copies:
         copy.wait()
 
-    held[...] = jnp.zeros_like(held)
     steps = plan[7, 0]
 
+    def powers(q):
+        terms_home = terms[plan[0, q * QUAD]]
+        fields = [pair_fields(plan, reals, q * QUAD + u) for u in range(QUAD)]
+        return [dot(terms_home, exponent_factors(places[f[0]], *f[2:])) for f in fields]
+
+    def hold(found):
+        for u in range(QUAD):
+            held[:, u * TILE : (u + 1) * TILE] = jnp.exp(found[u]).astype(BF16)
+
+    def products(q):
+        first = q * QUAD
+        across = [mapped[plan[2, first + u], tile_of(plan[1, first + u]), :] for u in range(QUAD)]
+        message[plan[0, first]] += dot(held[...], jnp.concatenate(across, axis=0))
+
     def step(q, carry):
-        now, ago = jnp.minimum(q, steps - 1) * QUAD, jnp.maximum(q - 1, 0) * QUAD
-        home = plan[0, now]
-        fields = [pair_fields(plan, reals, now + u) for u in range(QUAD)]
-        powers = [exponent(terms[home], places, f[0], *f[2:]) for f in fields]
-        across = [mapped[plan[2, ago + u], tile_of(plan[1, ago + u]), :] for u in range(QUAD)]
-        message[plan[0, ago]] += dot(held[...], jnp.concatenate(across, axis=0))
-        for u in range(QUAD):
-            held[:, u * TILE : (u + 1) * TILE] = jnp.exp(powers[u]).astype(BF16)
+        found = powers(q)
+        products(q - 1)
+        hold(found)
         return carry
 
-    lax.fori_loop(0, jnp.where(steps > 0, steps + 1, 0), step, 0)
+    @pl.when(steps > 0)
+    def _():
+        hold(powers(0))
+        lax.fori_loop(1, steps, step, 0)
+        products(steps - 1)
+
     for t in range(2):
         low = message[t].astype(BF16)
         for q in range(4):
@@ -259,7 +278,7 @@
     mixed = dot(packed, mixing[...])
     gate = jax.nn.sigmoid(mixed)
     slope = (readout[...] * gate * (1.0 + mixed * (1.0 - gate))).astype(BF16)
-    adjoint[...] = dot(slope, mixing[...], NT).astype(BF16).reshape(2, TILE, channels)
+    adjoint[...] = dot(slope, mixing[...], NT).astype(BF16)
     for t in range(2):
         flipped[t] = dot(mixing[...], slope[t * TILE : (t + 1) * TILE, :], NT).astype(BF16)
     half = channels // 2
@@ -284,9 +303,8 @@
 ):
     copies = fetch((hbm_plan, hbm_reals), (plan, reals), sems)
     kinds = radial.shape[0]
-    for t in range(2):
-        for k in range(kinds):
-            spread[t * kinds + k] = dot(radial[k], flipped[t]).astype(BF16)
+    for k in range(kinds):
+        spread[k] = dot(adjoint[...], radial[k], NT).astype(BF16)
 
     left_marks = (marks(1, 4, 8, 9), marks(2, 5, 10), marks(3, 6))
     right_marks = (marks(4), marks(5, 8), marks(6, 9, 10))
@@ -310,52 +328,69 @@
         both = jnp.concatenate([high, low], axis=0).astype(BF16)
         return jnp.concatenate([both, both], axis=1)
 
-    held[...] = jnp.zeros_like(held)
-    weights[...] = jnp.zeros_like(weights)
     steps = plan[7, 0]
 
+    def begin(q):
+        first = q * QUAD
+        home = plan[0, first]
+        fields = [pair_fields(plan, reals, first + u) for u in range(QUAD)]
+        tiles = [mapped[kind, tile_of(slot), :] for slot, kind, *_ in fields]
+        pulls = dot(jnp.concatenate(tiles, axis=0), flipped[home])
+        block = places[home]
+        powers = [
+            dot(terms[slot], exponent_factors(block, rate, [-x for x in shift], away))
+            for slot, _, rate, shift, away in fields
+        ]
+        return [(powers[u], pulls[u * TILE : (u + 1) * TILE], fields[u][2]) for u in range(QUAD)]
+
+    def hold(u, power, pull, rate):
+        kernel = jnp.exp(power)
+        held[u] = kernel.astype(BF16)
+        weight = (kernel * (-2.0 * rate)) * pull
+        high = weight.astype(BF16)
+        weights[u, 0] = high
+        weights[u, 1] = (weight - high.astype(F32)).astype(BF16)
+
+    def finish(q, u):
+        home = plan[0, q * QUAD]
+        slot, kind, _, shift, _ = pair_fields(plan, reals, q * QUAD + u)
+        left_shift = sum(left_marks[c] * shift[c] for c in range(3))
+        right_shift = sum(right_marks[c] * shift[c] for c in range(3))
+        far = monomials(slot, left_shift, right_shift)
+        near = monomials(home, -left_shift, -right_shift)
+        high, low = weights[u, 0], weights[u, 1]
+        sums[slot] += dot(near, jnp.concatenate([high, low], axis=1), NT)
+        grads[slot] += dot(held[u], spread[kind, tile_of(home), :])
+        return dot(far, jnp.concatenate([high, low], axis=0))
+
     def step(q, carry):
-        now, ago = jnp.minimum(q, steps - 1) * QUAD, jnp.maximum(q - 1, 0) * QUAD
-        home, home_ago = plan[0, now], plan[0, ago]
-        home_sum = None
+        found = begin(q)
+        parts = []
         for u in range(QUAD):
-            slot, kind, rate, shift, away = pair_fields(plan, reals, now + u)
-            power = exponent(terms[home], places, slot, rate, shift, away)
-            pull = dot(adjoint[home], mapped[kind, tile_of(slot), :], NT)
-
-            slot, kind, _, shift, _ = pair_fields(plan, reals, ago + u)
-            left_shift = sum(left_marks[c] * shift[c] for c in range(3))
-            right_shift = sum(right_marks[c] * shift[c] for c in range(3))
-            far = monomials(slot, left_shift, right_shift)
-            near = monomials(home_ago, -left_shift, -right_shift)
-            high, low = weights[u, 0], weights[u, 1]
-            part = dot(far, jnp.concatenate([high, low], axis=1), NT)
-            home_sum = part if home_sum is None else home_sum + part
-            sums[slot] += dot(near, jnp.concatenate([high, low], axis=0))
-            grads[slot] += dot(spread[home_ago * kinds + kind], held[u])
-
-            kernel = jnp.exp(power)
-            held[u] = kernel.astype(BF16)
-            weight = (kernel * (-2.0 * rate)) * pull
-            high = weight.astype(BF16)
-            weights[u, 0] = high
-            weights[u, 1] = (weight - high.astype(F32)).astype(BF16)
-        sums[home_ago] += home_sum
+            parts.append(finish(q - 1, u))
+            hold(u, *found[u])
+        sums[plan[0, (q - 1) * QUAD]] += sum(parts[1:], parts[0])
         return carry
 
-    lax.fori_loop(0, jnp.where(steps > 0, steps + 1, 0), step, 0)
-    back[0:TILE, :] = jnp.transpose(grads[2]).astype(BF16)
+    @pl.when(steps > 0)
+    def _():
+        for u, found in enumerate(begin(0)):
+            hold(u, *found)
+        lax.fori_loop(1, steps, step, 0)
+        parts = [finish(steps - 1, u) for u in range(QUAD)]
+        sums[plan[0, (steps - 1) * QUAD]] += sum(parts[1:], parts[0])
+
+    back[0:TILE, :] = grads[2].astype(BF16)
     tile_sums(sums[2], places[2], side)
     high, low = split(side[...])
     back[TILE : TILE + SIDE, 0:TILE] = high.astype(BF16)
     back[TILE : TILE + SIDE, TILE : 2 * TILE] = low.astype(BF16)
-    home_grads[...] = grads[0:2]
+    home_grads[...] = grads[0:2].reshape(home_grads.shape)
     home_sums[...] = sums[0:2]
 
 
-def own_kernel(home_grads, home_sums, places, own_grad, own_side, side):
+def own_kernel(home_sums, places, own_side, side):
     for t in range(2):
-        own_grad[t * TILE : (t + 1) * TILE, :] = jnp.transpose(home_grads[t])
         tile_sums(home_sums[t], places[t], side)
         own_side[:, t * TILE : (t + 1) * TILE] = side[...]
 
@@ -375,7 +410,7 @@
         payload[q * height + atoms : (q + 1) * height, :] = both
 
 
-def final_kernel(payload, grad, forces, virials):
+def final_kernel(payload, mixing_parts, grad, forces, virials, grad_mixing):
     atoms = grad.shape[0]
     height = atoms + 2 * SIDE
     total = None
@@ -389,9 +424,6 @@
     grad[...] = total.astype(BF16)
     forces[...] = side[0:3]
     virials[...] = side[8:14]
-
-
-def mixing_kernel(mixing_parts, grad_mixing):
     found = jnp.sum(mixing_parts[...], axis=0, keepdims=True)
     share = grad_mixing.shape[1]
     grad_mixing[0:1, :] = found[:, 0:share]
@@ -452,7 +484,7 @@
     )
     halo = hop(send, 1)
     lists = swap(lists, "rep")
-    rates, home_places, terms = call(
+    rates, home_places, home_terms = call(
         local_kernel,
         [((kinds, lanes), F32), ((2, 8, TILE), F32), ((2, TILE, DEPTH), BF16)],
         [decay, positions],
@@ -468,17 +500,17 @@
         flops=1 << 20,
     )
     tables = [smem((8, lanes), I32), smem((8, lanes), F32)]
-    mapped, places = call(
-        halo_kernel,
-        [((kinds, SLOTS * TILE, channels), BF16), ((SLOTS, 8, TILE), F32)],
-        [halo, home_places, radial, features],
-        flops=1 << 30,
-    )
-    [partial] = call(
+    mapped, places, terms, partial = call(
         forward_kernel,
-        [((reps * atoms, channels), BF16)],
-        [plan, reals, terms, mapped, places],
-        tables + [vmem((2, TILE, channels), F32), vmem((TILE, QUAD * TILE), BF16)],
+        [
+            ((kinds, SLOTS * TILE, channels), BF16),
+            ((SLOTS, 8, TILE), F32),
+            ((SLOTS, TILE, DEPTH), BF16),
+            ((reps * atoms, channels), BF16),
+        ],
+        [plan, reals, halo, home_places, home_terms, radial, features],
+        tables
+        + [vmem((TILE, TILE), F32), vmem((2, TILE, channels), F32), vmem((TILE, QUAD * TILE), BF16)],
         hbm=2,
         sems=2,
         flops=1 << 31,
@@ -486,19 +518,19 @@
     partial = swap(partial, "rep")
     adjoint, flipped, mixing_part = call(
         atom_kernel,
-        [((2, TILE, channels), BF16), ((2, channels, TILE), BF16), ((channels // 2, TILE), F32)],
+        [((atoms, channels), BF16), ((2, channels, TILE), BF16), ((channels // 2, TILE), F32)],
         [partial, mixing, readout.reshape(1, channels)],
         flops=1 << 28,
     )
     mixing_parts = swap(mixing_part, "dom")
-    back, home_grads, home_sums = call(
+    back, own_grad, home_sums = call(
         backward_kernel,
-        [((TILE + SIDE, channels), BF16), ((2, channels, TILE), F32), ((2, 2 * SIDE, TILE), F32)],
+        [((TILE + SIDE, channels), BF16), ((atoms, channels), F32), ((2, 2 * SIDE, TILE), F32)],
         [plan, reals, adjoint, flipped, places, terms, radial, mapped],
         tables
         + [
-            vmem((2 * kinds, channels, TILE), BF16),
-            vmem((SLOTS, channels, TILE), F32),
+            vmem((kinds, atoms, channels), BF16),
+            vmem((SLOTS, TILE, channels), F32),
             vmem((SLOTS, 2 * SIDE, TILE), F32),
             vmem((SLOTS, 2 * SIDE, TILE), F32),
             vmem((SIDE, TILE), F32),
@@ -510,12 +542,8 @@
         flops=1 << 33,
     )
     got = hop(back, -1)
-    own_grad, own_side = call(
-        own_kernel,
-        [((atoms, channels), F32), ((SIDE, atoms), F32)],
-        [home_grads, home_sums, places],
-        [vmem((SIDE, TILE), F32)],
-        flops=1 << 30,
+    [own_side] = call(
+        own_kernel, [((SIDE, atoms), F32)], [home_sums, places], [vmem((SIDE, TILE), F32)], flops=1 << 30
     )
     [payload] = call(
         return_kernel,
@@ -524,13 +552,13 @@
         flops=1 << 24,
     )
     payload = swap(payload, "rep")
-    [grad_mixing] = call(mixing_kernel, [((2, channels // reps), F32)], [mixing_parts])
-    grad, forces, virials = call(
-        final_kernel,
-        [((atoms, channels), BF16), ((3, atoms), F32), ((6, atoms), F32)],
-        [payload],
-    )
-    return grad, forces, virials, grad_mixing
+    return tuple(
+        call(
+            final_kernel,
+            [((atoms, channels), BF16), ((3, atoms), F32), ((6, atoms), F32), ((2, channels // reps), F32)],
+            [payload, mixing_parts],
+        )
+    )
 
 
 def solution(mesh):

time: 84.4 us -> 81.1 us (0.961); the launches traced: 82.9 us -> 80.8 us
  blocking collectives: 18.3 us -> 30.4 us
  waiting for transfers between devices: 14.3 us -> 8.74 us
  starting transfers between devices: 31.3 us -> 26.9 us
  Pallas kernels: 18.3 us -> 13.9 us
    all_to_all x1 -> x2, blocking collectives: 18.3 us -> 30.4 us  [swap(): return lax.all_to_all(array, axis, 0, 0, tiled=True)]
    all_to_all x3 -> x2, waiting for transfers between devices: 8.46 us -> 2.85 us  [swap(): return lax.all_to_all(array, axis, 0, 0, tiled=True)]
    all_to_all x3 -> x2, starting transfers between devices: 24.4 us -> 19.4 us  [swap(): return lax.all_to_all(array, axis, 0, 0, tiled=True)]
    pallas_call x11 -> x9, Pallas kernels: 18.3 us -> 13.9 us  [call(): pl.pallas_call(kernel, out_shape=[jax.ShapeDtypeStruct(shape, dtype) for...]
  transfers between devices with their start and end apart: 5 -> 4, of which waited for: 4 -> 3; matrix products, arithmetic and copies ran while one was open for 0% -> 0% of each run, Pallas kernels for 12% -> 8%
where the time goes in v3:
time: 81.1 us; the launch traced here: 80.8 us
  blocking collectives  30.4 us (37%)
  starting transfers between devices  26.9 us (33%)
  Pallas kernels  13.9 us (17%)
  waiting for transfers between devices  8.74 us (11%)
    all_to_all x2, blocking collectives, swap(): return lax.all_to_all(array, axis, 0, 0, tiled=True)  30.4 us
    all_to_all x2, starting transfers between devices, swap(): return lax.all_to_all(array, axis, 0, 0, tiled=True)  19.4 us
    pallas_call x9, Pallas kernels, call(): pl.pallas_call(kernel, out_shape=[jax.ShapeDtypeStruct(shape, dtype) for...  13.9 us
    ppermute x2, starting transfers between devices, hop(): return lax.ppermute(array, ('dom', 'rep'), ways)  7.57 us
    ppermute x2, waiting for transfers between devices, hop(): return lax.ppermute(array, ('dom', 'rep'), ways)  5.89 us
    all_to_all x2, waiting for transfers between devices, swap(): return lax.all_to_all(array, axis, 0, 0, tiled=True)  2.85 us
  transfers between devices with their start and end apart: 4, of which 3 were waited for; matrix products, arithmetic and copies ran while one was open for 0% of the time, Pallas kernels for 8%

profile of v3, /device:TPU:1, one launch (start us, length us, event | category | flops | bytes accessed | tf_op | source)
XLA Modules:
  0.0 80.8 jit_solution(2079588602261481303)
XLA Ops:
  0.6 0.0 copy-start.4
  0.6 0.0 copy-start.6
  0.7 1.9 %shard_map.138 = (bf16[144,256]{1,0:T(8,128)(2,1)}, s32[32,256]{1,0:T(8,128)}) custom-call(s32[4,128]{1,0:T(4,128)} %rows.1, s32[1,48]{1,0:T(1,128)} %bitcast.22, s32[1,48]{1,0:T(1,128)} %bitcast.23, s32[1,48]{1,0:T(1,128)} %bitcast.24, s32[3,48]{1,0:T(4,128)} %hbm_image.1, f32[3,256]{1,0:T(4,128)} %pos.1, bf16[256,256]{1,0:T(8,128)(2,1)} %feat.1), custom_call_target="tpu_custom_call" | custom-call | flops 1073741824 | bytes 1048576 | tf_op jit(solution)/shard_map/pallas_call | solution.py:436
  2.6 5.1 %all-to-all-start = ((s32[4,8,256]{2,1,0:T(8,128)}), s32[4,8,256]{2,1,0:T(8,128)S(1)}, u32[]{:S(2)}, u32[]{:S(2)}) async-start(s32[4,8,256]{2,1,0:T(8,128)} %bitcast.21), calls=%async_computation | async-start | bytes 65536 | tf_op jit(solution)/shard_map/all_to_all | solution.py:469
  7.7 0.0 copy-start.1
  7.7 0.0 copy-start.2
  7.7 4.1 %collective-permute-start = (bf16[144,256]{1,0:T(8,128)(2,1)}, bf16[144,256]{1,0:T(8,128)(2,1)S(1)}, u32[]{:S(2)}, u32[]{:S(2)}) collective-permute-start(bf16[144,256]{1,0:T(8,128)(2,1)} %get-tuple-element.25), channel_id=1, source_target_pairs={{0,4},{1,509},{2,10},{3,507},{4,8},{5,1},{6,14},{7,511},{8,12},{9,... | collective-permute-start | bytes 221192 | tf_op jit(solution)/shard_map/ppermute | solution.py:466
  11.8 0.0 copy-done.4
  11.8 0.0 copy-done.6
  11.8 0.7 shard_map.139
  12.5 0.0 all-to-all-done
  12.5 0.5 shard_map.140
  12.9 2.8 %collective-permute-done.halo = bf16[144,256]{1,0:T(8,128)(2,1)S(1)} collective-permute-done((bf16[144,256]{1,0:T(8,128)(2,1)}, bf16[144,256]{1,0:T(8,128)(2,1)S(1)}, u32[]{:S(2)}, u32[]{:S(2)}) %collective-permute-start) | collective-permute-done | bytes 73760 | tf_op jit(solution)/shard_map/ppermute | solution.py:466
  15.8 0.0 copy-done.1
  15.8 0.0 copy-done.2
  15.8 0.0 copy-start.3
  15.8 0.0 copy-start.5
  15.8 3.4 %shard_map.141 = (bf16[8,384,256]{2,1,0:T(8,128)(2,1)S(1)}, f32[3,8,128]{2,1,0:T(8,128)S(1)}, bf16[3,128,64]{2,1,0:T(8,128)(2,1)S(1)}, bf16[1024,256]{1,0:T(8,128)(2,1)S(1)}) custom-call(s32[8,256]{1,0:T(8,128)S(1)} %get-tuple-element.23.hbm_plan, f32[8,256]{1,0:T(8,128)S(1)} %get-tuple-element.24.hbm_reals, bf16[144,256]{1,0:T(8,128)(2,1)S(1)} %collective-permute-done.halo, ...), custom_call_target="tpu_custom_call" | custom-call | flops 2147483648 | bytes 1048576 | tf_op jit(solution)/shard_map/pallas_call | solution.py:436
  19.2 18.6 %all_to_all.44 = bf16[4,256,256]{2,1,0:T(8,128)(2,1)S(1)} all-to-all(bf16[4,256,256]{2,1,0:T(8,128)(2,1)S(1)} %bitcast.16), channel_id=1, replica_groups=mesh['dom'=128,'rep'=4] {'rep'}, dimensions={0} | all-to-all | bytes 1048576 | tf_op jit(solution)/shard_map/all_to_all | solution.py:469
  37.8 0.0 copy-done.3
  37.8 0.0 copy-done.5
  37.9 1.3 %shard_map.142 = (bf16[256,256]{1,0:T(8,128)(2,1)S(1)}, bf16[2,256,128]{2,1,0:T(8,128)(2,1)S(1)}, f32[128,128]{1,0:T(8,128)}) custom-call(bf16[1024,256]{1,0:T(8,128)(2,1)S(1)} %bitcast.17, bf16[256,256]{1,0:T(8,128)(2,1)S(1)} %copy-done.3, f32[1,256]{1,0:T(1,128)S(1)} %bitcast.20), custom_call_target="tpu_custom_call" | custom-call | flops 268435456 | bytes 1048576 | tf_op jit(solution)/shard_map/pallas_call | solution.py:436
  39.2 14.3 %all-to-all-start.3 = ((f32[128,1,128]{2,1,0:T(1,128)}), f32[128,1,128]{2,1,0:T(1,128)S(1)}, u32[]{:S(2)}, u32[]{:S(2)}) async-start(f32[128,1,128]{2,1,0:T(1,128)} %bitcast.11), calls=%async_computation.3 | async-start | bytes 131072 | tf_op jit(solution)/shard_map/all_to_all | solution.py:469
  53.5 5.2 %shard_map.143 = (bf16[144,256]{1,0:T(8,128)(2,1)S(1)}, f32[256,256]{1,0:T(8,128)S(1)}, f32[2,32,128]{2,1,0:T(8,128)S(1)}) custom-call(s32[8,256]{1,0:T(8,128)S(1)} %get-tuple-element.23.hbm_plan, f32[8,256]{1,0:T(8,128)S(1)} %get-tuple-element.24.hbm_reals, bf16[256,256]{1,0:T(8,128)(2,1)S(1)} %get-tuple-element.29.adjoint, ...), custom_call_target="tpu_custom_call" | custom-call | flops 8589934592 | bytes 1048576 | tf_op jit(solution)/shard_map/pallas_call | solution.py:436
  58.6 3.5 %collective-permute-start.1 = (bf16[144,256]{1,0:T(8,128)(2,1)S(1)}, bf16[144,256]{1,0:T(8,128)(2,1)S(1)}, u32[]{:S(2)}, u32[]{:S(2)}) collective-permute-start(bf16[144,256]{1,0:T(8,128)(2,1)S(1)} %get-tuple-element.34), channel_id=1, source_target_pairs={{0,508},{1,5},{2,506},{3,11},{4,0},{5,9},{6,510},{7,15},{8,4},{9,1... | collective-permute-start | bytes 221192 | tf_op jit(solution)/shard_map/ppermute | solution.py:466
  62.1 0.0 copy-start
  62.2 3.1 %collective-permute-done.1.got = bf16[144,256]{1,0:T(8,128)(2,1)S(1)} collective-permute-done((bf16[144,256]{1,0:T(8,128)(2,1)S(1)}, bf16[144,256]{1,0:T(8,128)(2,1)S(1)}, u32[]{:S(2)}, u32[]{:S(2)}) %collective-permute-start.1) | collective-permute-done | bytes 73760 | tf_op jit(solution)/shard_map/ppermute | solution.py:466
  65.2 0.0 copy-done
  65.2 0.2 shard_map.145
  65.4 2.9 %all-to-all-done.3 = f32[128,1,128]{2,1,0:T(1,128)S(1)} async-done(((f32[128,1,128]{2,1,0:T(1,128)}), f32[128,1,128]{2,1,0:T(1,128)S(1)}, u32[]{:S(2)}, u32[]{:S(2)}) %all-to-all-start.3) | async-done | bytes 65568 | tf_op jit(solution)/shard_map/all_to_all | solution.py:469
  68.3 11.7 %all_to_all.45 = bf16[4,288,256]{2,1,0:T(8,128)(2,1)S(1)} all-to-all(bf16[4,288,256]{2,1,0:T(8,128)(2,1)S(1)} %bitcast.14), channel_id=1, replica_groups=mesh['dom'=128,'rep'=4] {'rep'}, dimensions={0} | all-to-all | bytes 1179648 | tf_op jit(solution)/shard_map/all_to_all | solution.py:469
  80.0 0.8 shard_map.146
  (1 shorter events, 0.0 us)
Async XLA Ops:
  0.6 11.1 %copy-start.4 = (f32[3,256]{1,0:T(4,128)S(1)}, f32[3,256]{1,0:T(4,128)}, u32[]{:S(2)}) copy-start(f32[3,256]{1,0:T(4,128)} %pos.1) | copy-start | bytes 9220
  0.6 11.1 %copy-start.6 = (f32[8]{0:T(128)S(1)}, f32[8]{0:T(128)}, u32[]{:S(2)}) copy-start(f32[8]{0:T(128)} %hbm_decay.1) | copy-start | bytes 100
  2.6 9.9 %all-to-all-start = ((s32[4,8,256]{2,1,0:T(8,128)}), s32[4,8,256]{2,1,0:T(8,128)S(1)}, u32[]{:S(2)}, u32[]{:S(2)}) async-start(s32[4,8,256]{2,1,0:T(8,128)} %bitcast.21), calls=%async_computation | async-start | bytes 65536 | tf_op jit(solution)/shard_map/all_to_all | solution.py:469
  7.7 8.1 %copy-start.1 = (bf16[8,256,256]{2,1,0:T(8,128)(2,1)S(1)}, bf16[8,256,256]{2,1,0:T(8,128)(2,1)}, u32[]{:S(2)}) copy-start(bf16[8,256,256]{2,1,0:T(8,128)(2,1)} %radial.3) | copy-start | bytes 3145732
  7.7 8.1 %copy-start.2 = (bf16[256,256]{1,0:T(8,128)(2,1)S(1)}, bf16[256,256]{1,0:T(8,128)(2,1)}, u32[]{:S(2)}) copy-start(bf16[256,256]{1,0:T(8,128)(2,1)} %feat.1) | copy-start | bytes 393220
  7.7 8.1 %collective-permute-start = (bf16[144,256]{1,0:T(8,128)(2,1)}, bf16[144,256]{1,0:T(8,128)(2,1)S(1)}, u32[]{:S(2)}, u32[]{:S(2)}) collective-permute-start(bf16[144,256]{1,0:T(8,128)(2,1)} %get-tuple-element.25), channel_id=1, source_target_pairs={{0,4},{1,509},{2,10},{3,507},{4,8},{5,1},{6,14},{7,511},{8,12},{9,... | collective-permute-start | bytes 221192 | tf_op jit(solution)/shard_map/ppermute | solution.py:466
  15.8 22.1 %copy-start.3 = (bf16[256,256]{1,0:T(8,128)(2,1)S(1)}, bf16[256,256]{1,0:T(8,128)(2,1)}, u32[]{:S(2)}) copy-start(bf16[256,256]{1,0:T(8,128)(2,1)} %mixing.1) | copy-start | bytes 393220
  15.8 22.1 %copy-start.5 = (f32[256]{0:T(256)S(1)}, f32[256]{0:T(256)}, u32[]{:S(2)}) copy-start(f32[256]{0:T(256)} %param.15) | copy-start | bytes 3076
  39.2 29.1 %all-to-all-start.3 = ((f32[128,1,128]{2,1,0:T(1,128)}), f32[128,1,128]{2,1,0:T(1,128)S(1)}, u32[]{:S(2)}, u32[]{:S(2)}) async-start(f32[128,1,128]{2,1,0:T(1,128)} %bitcast.11), calls=%async_computation.3 | async-start | bytes 131072 | tf_op jit(solution)/shard_map/all_to_all | solution.py:469
  58.6 6.6 %collective-permute-start.1 = (bf16[144,256]{1,0:T(8,128)(2,1)S(1)}, bf16[144,256]{1,0:T(8,128)(2,1)S(1)}, u32[]{:S(2)}, u32[]{:S(2)}) collective-permute-start(bf16[144,256]{1,0:T(8,128)(2,1)S(1)} %get-tuple-element.34), channel_id=1, source_target_pairs={{0,508},{1,5},{2,506},{3,11},{4,0},{5,9},{6,510},{7,15},{8,4},{9,1... | collective-permute-start | bytes 221192 | tf_op jit(solution)/shard_map/ppermute | solution.py:466
  62.1 3.1 %copy-start = (s32[4,128]{1,0:T(4,128)S(1)}, s32[4,128]{1,0:T(4,128)}, u32[]{:S(2)}) copy-start(s32[4,128]{1,0:T(4,128)} %rows.1) | copy-start | bytes 6148

commit v4 on v3

--- a/solution.py
+++ b/solution.py
@@ -89,8 +89,12 @@
         lists[8 * q : 8 * q + 8, :] = block[...]
 
 
-def local_kernel(hbm_decay, pos, rates, places, terms, decay, wide, sems):
-    [copy] = fetch([hbm_decay], [decay], sems)
+def local_kernel(
+    hbm_decay, hbm_readout, hbm_rows, pos,
+    rates, places, terms, readout, rows,
+    decay, wide, sems,
+):
+    copy, *later = fetch([hbm_decay, hbm_readout, hbm_rows], [decay, readout, rows], sems)
     places[...] = jnp.zeros_like(places)
     wide[...] = jnp.zeros_like(wide)
     copy.wait()
@@ -99,6 +103,8 @@
     for t in range(2):
         places[t, 0:3, :] = pos[:, t * TILE : (t + 1) * TILE]
         terms[t] = tile_terms(places[t], wide)
+    for copy in later:
+        copy.wait()
 
 
 def plan_kernel(count, lists, rates, plan, reals):
@@ -109,10 +115,13 @@
     valid = jnp.where(iota((1, lanes), 1) < 4 * count, 1, 0)
     ahead = ones_where(iota((lanes, lanes), 0) < iota((lanes, lanes), 1))
 
-    def before(first, second):
-        both = jnp.where(iota((16, lanes), 0) < 8, first, second)
-        found = dot(both.astype(F32).astype(BF16), ahead).astype(I32)
-        return found[0:1, :], found[8:9, :]
+    def before(masks):
+        part = iota((16, lanes), 0) // 4
+        rows = masks[3]
+        for n in range(3):
+            rows = jnp.where(part == n, masks[n], rows)
+        found = dot(rows.astype(F32).astype(BF16), ahead).astype(I32)
+        return [found[4 * n : 4 * n + 1, :] for n in range(4)]
 
     def total(x):
         return jnp.sum(x.astype(F32), axis=1, keepdims=True).astype(I32)
@@ -124,16 +133,15 @@
         room = jnp.maximum(count - total(jnp.where(other == 2 + q, valid, 0)), 0)
         start = start + jnp.where(q < rep, room, 0)
         quota = quota + jnp.where(q == rep, room, 0)
-    turn, _ = before(local, local)
+    turn = before([local] * 4)[0]
     taken = jnp.where(turn >= start, local, 0) * jnp.where(turn < start + quota, 1, 0)
-    mine = taken + jnp.where(other == 2 + rep, valid, 0)
-    first = jnp.where(home == 0, mine, 0)
-    second = mine - first
-    place_first, place_second = before(first, second)
-    quads_first = (total(first) + (QUAD - 1)) // QUAD
-    quads_second = (total(second) + (QUAD - 1)) // QUAD
-    place = jnp.where(first > 0, place_first, place_second + quads_first * QUAD)
-    place = jnp.where(mine > 0, place, -1)
+    came = jnp.where(other == 2 + rep, valid, 0)
+    masks = [jnp.where(home == t, x, 0) for x in (came, taken) for t in range(2)]
+    place = jnp.full((1, lanes), -1, I32)
+    ends = [jnp.zeros((1, 1), I32)]
+    for mask, turn in zip(masks, before(masks)):
+        place = jnp.where(mask > 0, turn + ends[-1] * QUAD, place)
+        ends.append(ends[-1] + (total(mask) + (QUAD - 1)) // QUAD)
     put = ones_where(iota((lanes, lanes), 0) == place)
     row = iota((8, lanes), 0)
     fields = jnp.where(row == 1, jnp.minimum(table, 2), table)
@@ -148,7 +156,7 @@
     fields = jnp.concatenate([fields, rate], axis=0).astype(BF16)
     listed = dot(fields, put, NT)
     counts = listed[0:8, :].astype(I32)
-    plan[...] = jnp.where(row == 7, quads_first + quads_second, counts)
+    plan[...] = jnp.where(row == 3, ends[2], jnp.where(row == 4, ends[4], counts))
     rate = listed[8:9, :] + listed[9:10, :] + listed[10:11, :]
     empty = 1.0 - listed[6:7, :]
     reals[...] = jnp.where(row == 0, rate + empty, jnp.where(row == 7, empty * FAR, listed[0:8, :] * EDGE))
@@ -188,53 +196,76 @@
     return jnp.transpose(wide[...]).astype(BF16)[:, 0:DEPTH]
 
 
-def forward_kernel(
-    hbm_plan, hbm_reals, halo, home_places, home_terms, radial, feat,
+def forward_groups(plan, reals, first, last, terms, places_of, mapped_of, message, held):
+    def powers(q):
+        terms_home = terms[plan[0, q * QUAD]]
+        fields = [pair_fields(plan, reals, q * QUAD + u) for u in range(QUAD)]
+        return [dot(terms_home, exponent_factors(places_of(f[0]), *f[2:])) for f in fields]
+
+    def hold(found):
+        for u in range(QUAD):
+            held[:, u * TILE : (u + 1) * TILE] = jnp.exp(found[u]).astype(BF16)
+
+    def products(q):
+        at = q * QUAD
+        across = [mapped_of(plan[2, at + u], plan[1, at + u]) for u in range(QUAD)]
+        message[plan[0, at]] += dot(held[...], jnp.concatenate(across, axis=0))
+
+    def step(q, carry):
+        found = powers(q)
+        products(q - 1)
+        hold(found)
+        return carry
+
+    @pl.when(last > first)
+    def _():
+        hold(powers(first))
+        lax.fori_loop(first + 1, last, step, 0)
+        products(last - 1)
+
+
+def home_forward_kernel(
+    hbm_plan, hbm_reals, home_places, home_terms, radial, feat,
+    home_mapped, message,
+    plan, reals, held, sems,
+):
+    copies = fetch((hbm_plan, hbm_reals), (plan, reals), sems)
+    for k in range(radial.shape[0]):
+        home_mapped[k] = dot(feat[...], radial[k]).astype(BF16)
+    message[...] = jnp.zeros_like(message)
+    for copy in copies:
+        copy.wait()
+    forward_groups(
+        plan, reals, plan[3, 0], plan[4, 0], home_terms,
+        lambda slot: home_places[slot],
+        lambda kind, slot: home_mapped[kind, tile_of(slot), :],
+        message, held,
+    )
+
+
+def halo_forward_kernel(
+    hbm_plan, hbm_reals, halo, home_places, home_terms, radial, home_message,
     mapped, places, terms, partial,
     plan, reals, wide, message, held, sems,
 ):
     copies = fetch((hbm_plan, hbm_reals), (plan, reals), sems)
-    atoms = feat.shape[0]
     places[0:2] = home_places[...]
     places[2] = halo_places(halo)
     terms[0:2] = home_terms[...]
     wide[...] = jnp.zeros_like(wide)
     terms[2] = tile_terms(places[2], wide)
     for k in range(radial.shape[0]):
-        mapped[k, 0:atoms, :] = dot(feat[...], radial[k]).astype(BF16)
-        mapped[k, atoms : atoms + TILE, :] = dot(halo[0:TILE, :], radial[k]).astype(BF16)
-    message[...] = jnp.zeros_like(message)
+        mapped[k] = dot(halo[0:TILE, :], radial[k]).astype(BF16)
+    message[...] = home_message[...]
     for copy in copies:
         copy.wait()
-
-    steps = plan[7, 0]
-
-    def powers(q):
-        terms_home = terms[plan[0, q * QUAD]]
-        fields = [pair_fields(plan, reals, q * QUAD + u) for u in range(QUAD)]
-        return [dot(terms_home, exponent_factors(places[f[0]], *f[2:])) for f in fields]
-
-    def hold(found):
-        for u in range(QUAD):
-            held[:, u * TILE : (u + 1) * TILE] = jnp.exp(found[u]).astype(BF16)
-
-    def products(q):
-        first = q * QUAD
-        across = [mapped[plan[2, first + u], tile_of(plan[1, first + u]), :] for u in range(QUAD)]
-        message[plan[0, first]] += dot(held[...], jnp.concatenate(across, axis=0))
-
-    def step(q, carry):
-        found = powers(q)
-        products(q - 1)
-        hold(found)
-        return carry
-
-    @pl.when(steps > 0)
-    def _():
-        hold(powers(0))
-        lax.fori_loop(1, steps, step, 0)
-        products(steps - 1)
-
+    forward_groups(
+        plan, reals, 0, plan[3, 0], home_terms,
+        lambda slot: places[2],
+        lambda kind, slot: mapped[kind],
+        message, held,
+    )
+    atoms = 2 * TILE
     for t in range(2):
         low = message[t].astype(BF16)
         for q in range(4):
@@ -296,31 +327,23 @@
     mixing_part[...] = gradient
 
 
-def backward_kernel(
-    hbm_plan, hbm_reals, adjoint, flipped, places, terms, radial, mapped,
-    back, home_grads, home_sums,
-    plan, reals, spread, grads, bases, sums, side, held, weights, sems,
-):
-    copies = fetch((hbm_plan, hbm_reals), (plan, reals), sems)
-    kinds = radial.shape[0]
-    for k in range(kinds):
-        spread[k] = dot(adjoint[...], radial[k], NT).astype(BF16)
-
-    left_marks = (marks(1, 4, 8, 9), marks(2, 5, 10), marks(3, 6))
-    right_marks = (marks(4), marks(5, 8), marks(6, 9, 10))
-    left_one, right_one = marks(0), marks(0, 1, 2, 3)
-    for t in range(SLOTS):
-        block = places[t]
-        left, right = left_one, right_one
-        for c in range(3):
-            left = left + left_marks[c] * block[c : c + 1, :]
-            right = right + right_marks[c] * block[c : c + 1, :]
-        bases[t, 0:SIDE, :] = left
-        bases[t, SIDE : 2 * SIDE, :] = right
-    sums[...] = jnp.zeros_like(sums)
-    grads[...] = jnp.zeros_like(grads)
-    for copy in copies:
-        copy.wait()
+def tile_bases(block):
+    left, right = marks(0), marks(0, 1, 2, 3)
+    for c in range(3):
+        left = left + LEFT_MARKS[c]() * block[c : c + 1, :]
+        right = right + RIGHT_MARKS[c]() * block[c : c + 1, :]
+    return jnp.concatenate([left, right], axis=0)
+
+
+LEFT_MARKS = tuple(functools.partial(marks, *x) for x in ((1, 4, 8, 9), (2, 5, 10), (3, 6)))
+RIGHT_MARKS = tuple(functools.partial(marks, *x) for x in ((4,), (5, 8), (6, 9, 10)))
+
+
+def backward_groups(
+    plan, reals, first, last, flipped, places, terms, spread, bases, mapped_of, tile_at, grads, sums, held, weights
+):
+    left_marks = [f() for f in LEFT_MARKS]
+    right_marks = [f() for f in RIGHT_MARKS]
 
     def monomials(t, left_shift, right_shift):
         base = bases[t]
@@ -328,13 +351,11 @@
         both = jnp.concatenate([high, low], axis=0).astype(BF16)
         return jnp.concatenate([both, both], axis=1)
 
-    steps = plan[7, 0]
-
     def begin(q):
-        first = q * QUAD
-        home = plan[0, first]
-        fields = [pair_fields(plan, reals, first + u) for u in range(QUAD)]
-        tiles = [mapped[kind, tile_of(slot), :] for slot, kind, *_ in fields]
+        at = q * QUAD
+        home = plan[0, at]
+        fields = [pair_fields(plan, reals, at + u) for u in range(QUAD)]
+        tiles = [mapped_of(kind, slot) for slot, kind, *_ in fields]
         pulls = dot(jnp.concatenate(tiles, axis=0), flipped[home])
         block = places[home]
         powers = [
@@ -360,7 +381,7 @@
         near = monomials(home, -left_shift, -right_shift)
         high, low = weights[u, 0], weights[u, 1]
         sums[slot] += dot(near, jnp.concatenate([high, low], axis=1), NT)
-        grads[slot] += dot(held[u], spread[kind, tile_of(home), :])
+        grads[tile_at(slot), :] += dot(held[u], spread[kind, tile_of(home), :])
         return dot(far, jnp.concatenate([high, low], axis=0))
 
     def step(q, carry):
@@ -372,26 +393,61 @@
         sums[plan[0, (q - 1) * QUAD]] += sum(parts[1:], parts[0])
         return carry
 
-    @pl.when(steps > 0)
+    @pl.when(last > first)
     def _():
-        for u, found in enumerate(begin(0)):
+        for u, found in enumerate(begin(first)):
             hold(u, *found)
-        lax.fori_loop(1, steps, step, 0)
-        parts = [finish(steps - 1, u) for u in range(QUAD)]
-        sums[plan[0, (steps - 1) * QUAD]] += sum(parts[1:], parts[0])
-
-    back[0:TILE, :] = grads[2].astype(BF16)
+        lax.fori_loop(first + 1, last, step, 0)
+        parts = [finish(last - 1, u) for u in range(QUAD)]
+        sums[plan[0, (last - 1) * QUAD]] += sum(parts[1:], parts[0])
+
+
+def halo_backward_kernel(
+    hbm_plan, hbm_reals, adjoint, flipped, places, terms, radial, mapped,
+    back, spread, bases, home_sums,
+    plan, reals, grads, sums, side, held, weights, sems,
+):
+    copies = fetch((hbm_plan, hbm_reals), (plan, reals), sems)
+    for k in range(radial.shape[0]):
+        spread[k] = dot(adjoint[...], radial[k], NT).astype(BF16)
+    for t in range(SLOTS):
+        bases[t] = tile_bases(places[t])
+    sums[...] = jnp.zeros_like(sums)
+    grads[...] = jnp.zeros_like(grads)
+    for copy in copies:
+        copy.wait()
+    backward_groups(
+        plan, reals, 0, plan[3, 0], flipped, places, terms, spread, bases,
+        lambda kind, slot: mapped[kind],
+        lambda slot: slice(0, TILE),
+        grads, sums, held, weights,
+    )
+    back[0:TILE, :] = grads[...].astype(BF16)
     tile_sums(sums[2], places[2], side)
     high, low = split(side[...])
     back[TILE : TILE + SIDE, 0:TILE] = high.astype(BF16)
     back[TILE : TILE + SIDE, TILE : 2 * TILE] = low.astype(BF16)
-    home_grads[...] = grads[0:2].reshape(home_grads.shape)
     home_sums[...] = sums[0:2]
 
 
-def own_kernel(home_sums, places, own_side, side):
+def home_backward_kernel(
+    hbm_plan, hbm_reals, flipped, places, terms, home_mapped, spread, bases, home_sums,
+    own_grad, own_side,
+    plan, reals, sums, side, held, weights, sems,
+):
+    copies = fetch((hbm_plan, hbm_reals), (plan, reals), sems)
+    sums[...] = home_sums[...]
+    own_grad[...] = jnp.zeros_like(own_grad)
+    for copy in copies:
+        copy.wait()
+    backward_groups(
+        plan, reals, plan[3, 0], plan[4, 0], flipped, places, terms, spread, bases,
+        lambda kind, slot: home_mapped[kind, tile_of(slot), :],
+        tile_of,
+        own_grad, sums, held, weights,
+    )
     for t in range(2):
-        tile_sums(home_sums[t], places[t], side)
+        tile_sums(sums[t], places[t], side)
         own_side[:, t * TILE : (t + 1) * TILE] = side[...]
 
 
@@ -454,7 +510,7 @@
     doms, reps = lax.axis_size("dom"), lax.axis_size("rep")
     lanes = 2 * TILE
     height = atoms + 2 * SIDE
-    assert reps == len(OFFSETS) and atoms == 2 * TILE and 4 * count <= lanes - 4 * QUAD
+    assert reps == len(OFFSETS) and atoms == 2 * TILE and 4 * count + 4 * QUAD <= lanes
     assert channels == 2 * doms
 
     def hop(array, sign):
@@ -484,13 +540,19 @@
     )
     halo = hop(send, 1)
     lists = swap(lists, "rep")
-    rates, home_places, home_terms = call(
+    rates, home_places, home_terms, readout, send_rows = call(
         local_kernel,
-        [((kinds, lanes), F32), ((2, 8, TILE), F32), ((2, TILE, DEPTH), BF16)],
-        [decay, positions],
+        [
+            ((kinds, lanes), F32),
+            ((2, 8, TILE), F32),
+            ((2, TILE, DEPTH), BF16),
+            ((1, channels), F32),
+            (send_rows.shape, I32),
+        ],
+        [decay, readout.reshape(1, channels), send_rows, positions],
         [smem(decay.shape, F32), vmem((TILE, TILE), F32)],
-        hbm=1,
-        sems=1,
+        hbm=3,
+        sems=3,
         flops=1 << 32,
     )
     plan, reals = call(
@@ -500,15 +562,24 @@
         flops=1 << 20,
     )
     tables = [smem((8, lanes), I32), smem((8, lanes), F32)]
+    home_mapped, message = call(
+        home_forward_kernel,
+        [((kinds, atoms, channels), BF16), ((2, TILE, channels), F32)],
+        [plan, reals, home_places, home_terms, radial, features],
+        tables + [vmem((TILE, QUAD * TILE), BF16)],
+        hbm=2,
+        sems=2,
+        flops=1 << 32,
+    )
     mapped, places, terms, partial = call(
-        forward_kernel,
+        halo_forward_kernel,
         [
-            ((kinds, SLOTS * TILE, channels), BF16),
+            ((kinds, TILE, channels), BF16),
             ((SLOTS, 8, TILE), F32),
             ((SLOTS, TILE, DEPTH), BF16),
             ((reps * atoms, channels), BF16),
         ],
-        [plan, reals, halo, home_places, home_terms, radial, features],
+        [plan, reals, halo, home_places, home_terms, radial, message],
         tables
         + [vmem((TILE, TILE), F32), vmem((2, TILE, channels), F32), vmem((TILE, QUAD * TILE), BF16)],
         hbm=2,
@@ -519,31 +590,34 @@
     adjoint, flipped, mixing_part = call(
         atom_kernel,
         [((atoms, channels), BF16), ((2, channels, TILE), BF16), ((channels // 2, TILE), F32)],
-        [partial, mixing, readout.reshape(1, channels)],
+        [partial, mixing, readout],
         flops=1 << 28,
     )
     mixing_parts = swap(mixing_part, "dom")
-    back, own_grad, home_sums = call(
-        backward_kernel,
-        [((TILE + SIDE, channels), BF16), ((atoms, channels), F32), ((2, 2 * SIDE, TILE), F32)],
+    group_space = [vmem((SIDE, TILE), F32), vmem((QUAD, TILE, TILE), BF16), vmem((QUAD, 2, TILE, TILE), BF16)]
+    back, spread, bases, home_sums = call(
+        halo_backward_kernel,
+        [
+            ((TILE + SIDE, channels), BF16),
+            ((kinds, atoms, channels), BF16),
+            ((SLOTS, 2 * SIDE, TILE), F32),
+            ((2, 2 * SIDE, TILE), F32),
+        ],
         [plan, reals, adjoint, flipped, places, terms, radial, mapped],
-        tables
-        + [
-            vmem((kinds, atoms, channels), BF16),
-            vmem((SLOTS, TILE, channels), F32),
-            vmem((SLOTS, 2 * SIDE, TILE), F32),
-            vmem((SLOTS, 2 * SIDE, TILE), F32),
-            vmem((SIDE, TILE), F32),
-            vmem((QUAD, TILE, TILE), BF16),
-            vmem((QUAD, 2, TILE, TILE), BF16),
-        ],
+        tables + [vmem((TILE, channels), F32), vmem((SLOTS, 2 * SIDE, TILE), F32)] + group_space,
         hbm=2,
         sems=2,
         flops=1 << 33,
     )
     got = hop(back, -1)
-    [own_side] = call(
-        own_kernel, [((SIDE, atoms), F32)], [home_sums, places], [vmem((SIDE, TILE), F32)], flops=1 << 30
+    own_grad, own_side = call(
+        home_backward_kernel,
+        [((atoms, channels), F32), ((SIDE, atoms), F32)],
+        [plan, reals, flipped, places, terms, home_mapped, spread, bases, home_sums],
+        tables + [vmem((2, 2 * SIDE, TILE), F32)] + group_space,
+        hbm=2,
+        sems=2,
+        flops=1 << 32,
     )
     [payload] = call(
         return_kernel,

time: 81.1 us -> 82 us (1.011)
  Pallas kernels: 13.9 us -> 18.2 us
  starting transfers between devices: 26.9 us -> 23.5 us
  waiting for transfers between devices: 8.74 us -> 5.67 us
  blocking collectives: 30.4 us -> 32.7 us
    pallas_call x9 -> x10, Pallas kernels: 13.9 us -> 18.2 us  [call(): pl.pallas_call(kernel, out_shape=[jax.ShapeDtypeStruct(shape, dtype) for...]
    ppermute x2, waiting for transfers between devices: 5.89 us -> 2.66 us  [hop(): return lax.ppermute(array, ('dom', 'rep'), ways)]
    all_to_all x2, blocking collectives: 30.4 us -> 32.7 us  [swap(): return lax.all_to_all(array, axis, 0, 0, tiled=True)]
    all_to_all x2, starting transfers between devices: 19.4 us -> 17.5 us  [swap(): return lax.all_to_all(array, axis, 0, 0, tiled=True)]
    ppermute x2, starting transfers between devices: 7.57 us -> 6.01 us  [hop(): return lax.ppermute(array, ('dom', 'rep'), ways)]
  transfers between devices with their start and end apart: 4 -> 4, of which waited for: 3 -> 3; matrix products, arithmetic and copies ran while one was open for 0% -> 0% of each run, Pallas kernels for 8% -> 14%
where the time goes in v4:
time: 82 us; the launch traced here: 80.9 us
  blocking collectives  32.7 us (40%)
  starting transfers between devices  23.5 us (29%)
  Pallas kernels  18.2 us (22%)
  waiting for transfers between devices  5.67 us (7%)
    all_to_all x2, blocking collectives, swap(): return lax.all_to_all(array, axis, 0, 0, tiled=True)  32.7 us
    pallas_call x10, Pallas kernels, call(): pl.pallas_call(kernel, out_shape=[jax.ShapeDtypeStruct(shape, dtype) for...  18.2 us
    all_to_all x2, starting transfers between devices, swap(): return lax.all_to_all(array, axis, 0, 0, tiled=True)  17.5 us
    ppermute x2, starting transfers between devices, hop(): return lax.ppermute(array, ('dom', 'rep'), ways)  6.01 us
    all_to_all x2, waiting for transfers between devices, swap(): return lax.all_to_all(array, axis, 0, 0, tiled=True)  3.01 us
    ppermute x2, waiting for transfers between devices, hop(): return lax.ppermute(array, ('dom', 'rep'), ways)  2.66 us
  transfers between devices with their start and end apart: 4, of which 3 were waited for; matrix products, arithmetic and copies ran while one was open for 0% of the time, Pallas kernels for 14%

profile of v4, /device:TPU:1, one launch (start us, length us, event | category | flops | bytes accessed | tf_op | source)
XLA Modules:
  0.0 80.9 jit_solution(7048073310878764361)
XLA Ops:
  0.6 1.9 %shard_map.139 = (bf16[144,256]{1,0:T(8,128)(2,1)}, s32[32,256]{1,0:T(8,128)}) custom-call(s32[4,128]{1,0:T(4,128)} %hbm_rows.3, s32[1,48]{1,0:T(1,128)} %bitcast.22, s32[1,48]{1,0:T(1,128)} %bitcast.23, s32[1,48]{1,0:T(1,128)} %bitcast.24, s32[3,48]{1,0:T(4,128)} %hbm_image.1, f32[3,256]{1,0:T(4,128)} %hbm_pos.1, bf16[256,256]{1,0:T(8,128)(2,1)} %feat.1), custom_call_target="tpu_custom_call" | custom-call | flops 1073741824 | bytes 1048576 | tf_op jit(solution)/shard_map/pallas_call | solution.py:492
  2.6 0.0 copy-start.3
  2.6 5.1 %all-to-all-start = ((s32[4,8,256]{2,1,0:T(8,128)}), s32[4,8,256]{2,1,0:T(8,128)S(1)}, u32[]{:S(2)}, u32[]{:S(2)}) async-start(s32[4,8,256]{2,1,0:T(8,128)} %bitcast.21), calls=%async_computation | async-start | bytes 65536 | tf_op jit(solution)/shard_map/all_to_all | solution.py:525
  7.7 0.0 copy-start.4
  7.7 0.0 copy-start.5
  7.7 0.0 copy-start.6
  7.7 4.1 %collective-permute-start = (bf16[144,256]{1,0:T(8,128)(2,1)}, bf16[144,256]{1,0:T(8,128)(2,1)S(1)}, u32[]{:S(2)}, u32[]{:S(2)}) collective-permute-start(bf16[144,256]{1,0:T(8,128)(2,1)} %get-tuple-element.33), channel_id=1, source_target_pairs={{0,4},{1,509},{2,10},{3,507},{4,8},{5,1},{6,14},{7,511},{8,12},{9,... | collective-permute-start | bytes 221192 | tf_op jit(solution)/shard_map/ppermute | solution.py:522
  11.8 0.0 copy-done.3
  11.8 0.0 copy-done.4
  11.8 0.0 copy-done.5
  11.8 0.0 copy-done.6
  11.8 0.0 copy-start
  11.8 0.0 copy-start.1
  11.8 0.7 shard_map.138
  12.5 0.0 all-to-all-done
  12.5 0.5 shard_map.140
  13.0 0.0 copy-done
  13.0 0.0 copy-done.1
  13.0 1.7 %shard_map.141 = (bf16[8,256,256]{2,1,0:T(8,128)(2,1)S(1)}, f32[2,128,256]{2,1,0:T(8,128)S(1)}) custom-call(s32[8,256]{1,0:T(8,128)S(1)} %get-tuple-element.31.hbm_plan, f32[8,256]{1,0:T(8,128)S(1)} %get-tuple-element.32.hbm_reals, f32[2,8,128]{2,1,0:T(8,128)S(1)} %get-tuple-element.34.home_places, bf16[2,128,64]{2,1,0:T(8,128)(2,1)S(1)} %get-tuple-element.35.home_terms, ...), custom_call_target="tpu_custom_call" | custom-call | flops 4294967296 | bytes 1048576 | tf_op jit(solution)/shard_map/pallas_call | solution.py:492
  14.7 1.0 %collective-permute-done.halo = bf16[144,256]{1,0:T(8,128)(2,1)S(1)} collective-permute-done((bf16[144,256]{1,0:T(8,128)(2,1)}, bf16[144,256]{1,0:T(8,128)(2,1)S(1)}, u32[]{:S(2)}, u32[]{:S(2)}) %collective-permute-start) | collective-permute-done | bytes 73760 | tf_op jit(solution)/shard_map/ppermute | solution.py:522
  15.8 3.1 %shard_map.142 = (bf16[8,128,256]{2,1,0:T(8,128)(2,1)S(1)}, f32[3,8,128]{2,1,0:T(8,128)S(1)}, bf16[3,128,64]{2,1,0:T(8,128)(2,1)S(1)}, bf16[1024,256]{1,0:T(8,128)(2,1)S(1)}) custom-call(s32[8,256]{1,0:T(8,128)S(1)} %get-tuple-element.31.hbm_plan, f32[8,256]{1,0:T(8,128)S(1)} %get-tuple-element.32.hbm_reals, bf16[144,256]{1,0:T(8,128)(2,1)S(1)} %collective-permute-done.halo, ...), custom_call_target="tpu_custom_call" | custom-call | flops 2147483648 | bytes 1048576 | tf_op jit(solution)/shard_map/pallas_call | solution.py:492
  18.9 0.0 copy-start.2
  18.9 20.0 %all_to_all.44 = bf16[4,256,256]{2,1,0:T(8,128)(2,1)S(1)} all-to-all(bf16[4,256,256]{2,1,0:T(8,128)(2,1)S(1)} %bitcast.16), channel_id=1, replica_groups=mesh['dom'=128,'rep'=4] {'rep'}, dimensions={0} | all-to-all | bytes 1048576 | tf_op jit(solution)/shard_map/all_to_all | solution.py:525
  38.9 0.0 copy-done.2
  38.9 1.3 %shard_map.143 = (bf16[256,256]{1,0:T(8,128)(2,1)S(1)}, bf16[2,256,128]{2,1,0:T(8,128)(2,1)S(1)}, f32[128,128]{1,0:T(8,128)}) custom-call(bf16[1024,256]{1,0:T(8,128)(2,1)S(1)} %bitcast.17, bf16[256,256]{1,0:T(8,128)(2,1)S(1)} %copy-done.2, f32[1,256]{1,0:T(1,128)S(1)} %get-tuple-element.38.readout), custom_call_target="tpu_custom_call" | custom-call | flops 268435456 | bytes 1048576 | tf_op jit(solution)/shard_map/pallas_call | solution.py:492
  40.2 12.4 %all-to-all-start.3 = ((f32[128,1,128]{2,1,0:T(1,128)}), f32[128,1,128]{2,1,0:T(1,128)S(1)}, u32[]{:S(2)}, u32[]{:S(2)}) async-start(f32[128,1,128]{2,1,0:T(1,128)} %bitcast.11), calls=%async_computation.3 | async-start | bytes 131072 | tf_op jit(solution)/shard_map/all_to_all | solution.py:525
  52.6 5.6 %shard_map.144 = (bf16[144,256]{1,0:T(8,128)(2,1)S(1)}, bf16[8,256,256]{2,1,0:T(8,128)(2,1)S(1)}, f32[3,32,128]{2,1,0:T(8,128)S(1)}, f32[2,32,128]{2,1,0:T(8,128)S(1)}) custom-call(s32[8,256]{1,0:T(8,128)S(1)} %get-tuple-element.31.hbm_plan, f32[8,256]{1,0:T(8,128)S(1)} %get-tuple-element.32.hbm_reals, bf16[256,256]{1,0:T(8,128)(2,1)S(1)} %get-tuple-element.39.adjoint, ...), custom_call_target="tpu_custom_call" | custom-call | flops 8589934592 | bytes 1048576 | tf_op jit(solution)/shard_map/pallas_call | solution.py:492
  58.2 1.9 %collective-permute-start.1 = (bf16[144,256]{1,0:T(8,128)(2,1)S(1)}, bf16[144,256]{1,0:T(8,128)(2,1)S(1)}, u32[]{:S(2)}, u32[]{:S(2)}) collective-permute-start(bf16[144,256]{1,0:T(8,128)(2,1)S(1)} %get-tuple-element.44), channel_id=1, source_target_pairs={{0,508},{1,5},{2,506},{3,11},{4,0},{5,9},{6,510},{7,15},{8,4},{9,1... | collective-permute-start | bytes 221192 | tf_op jit(solution)/shard_map/ppermute | solution.py:522
  60.1 2.4 %shard_map.145 = (f32[256,256]{1,0:T(8,128)S(1)}, f32[16,256]{1,0:T(8,128)S(1)}) custom-call(s32[8,256]{1,0:T(8,128)S(1)} %get-tuple-element.31.hbm_plan, f32[8,256]{1,0:T(8,128)S(1)} %get-tuple-element.32.hbm_reals, bf16[2,256,128]{2,1,0:T(8,128)(2,1)S(1)} %get-tuple-element.40.flipped, f32[3,8,128]{2,1,0:T(8,128)S(1)} %get-tuple-element.41.places, ...), custom_call_target="tpu_custom_call" | custom-call | flops 4294967296 | bytes 1048576 | tf_op jit(solution)/shard_map/pallas_call | solution.py:492
  62.6 1.6 %collective-permute-done.1.got = bf16[144,256]{1,0:T(8,128)(2,1)S(1)} collective-permute-done((bf16[144,256]{1,0:T(8,128)(2,1)S(1)}, bf16[144,256]{1,0:T(8,128)(2,1)S(1)}, u32[]{:S(2)}, u32[]{:S(2)}) %collective-permute-start.1) | collective-permute-done | bytes 73760 | tf_op jit(solution)/shard_map/ppermute | solution.py:522
  64.2 0.2 shard_map.146
  64.4 3.0 %all-to-all-done.3 = f32[128,1,128]{2,1,0:T(1,128)S(1)} async-done(((f32[128,1,128]{2,1,0:T(1,128)}), f32[128,1,128]{2,1,0:T(1,128)S(1)}, u32[]{:S(2)}, u32[]{:S(2)}) %all-to-all-start.3) | async-done | bytes 65568 | tf_op jit(solution)/shard_map/all_to_all | solution.py:525
  67.4 12.7 %all_to_all.45 = bf16[4,288,256]{2,1,0:T(8,128)(2,1)S(1)} all-to-all(bf16[4,288,256]{2,1,0:T(8,128)(2,1)S(1)} %bitcast.14), channel_id=1, replica_groups=mesh['dom'=128,'rep'=4] {'rep'}, dimensions={0} | all-to-all | bytes 1179648 | tf_op jit(solution)/shard_map/all_to_all | solution.py:525
  80.2 0.8 shard_map.147
Async XLA Ops:
  2.6 9.2 %copy-start.3 = (f32[3,256]{1,0:T(4,128)S(1)}, f32[3,256]{1,0:T(4,128)}, u32[]{:S(2)}) copy-start(f32[3,256]{1,0:T(4,128)} %hbm_pos.1) | copy-start | bytes 9220
  2.6 10.0 %all-to-all-start = ((s32[4,8,256]{2,1,0:T(8,128)}), s32[4,8,256]{2,1,0:T(8,128)S(1)}, u32[]{:S(2)}, u32[]{:S(2)}) async-start(s32[4,8,256]{2,1,0:T(8,128)} %bitcast.21), calls=%async_computation | async-start | bytes 65536 | tf_op jit(solution)/shard_map/all_to_all | solution.py:525
  7.7 4.1 %copy-start.4 = (s32[4,128]{1,0:T(4,128)S(1)}, s32[4,128]{1,0:T(4,128)}, u32[]{:S(2)}) copy-start(s32[4,128]{1,0:T(4,128)} %hbm_rows.3) | copy-start | bytes 6148
  7.7 4.1 %copy-start.5 = (f32[256]{0:T(256)S(1)}, f32[256]{0:T(256)}, u32[]{:S(2)}) copy-start(f32[256]{0:T(256)} %param.15) | copy-start | bytes 3076
  7.7 4.1 %copy-start.6 = (f32[8]{0:T(128)S(1)}, f32[8]{0:T(128)}, u32[]{:S(2)}) copy-start(f32[8]{0:T(128)} %hbm_decay.1) | copy-start | bytes 100
  7.7 8.1 %collective-permute-start = (bf16[144,256]{1,0:T(8,128)(2,1)}, bf16[144,256]{1,0:T(8,128)(2,1)S(1)}, u32[]{:S(2)}, u32[]{:S(2)}) collective-permute-start(bf16[144,256]{1,0:T(8,128)(2,1)} %get-tuple-element.33), channel_id=1, source_target_pairs={{0,4},{1,509},{2,10},{3,507},{4,8},{5,1},{6,14},{7,511},{8,12},{9,... | collective-permute-start | bytes 221192 | tf_op jit(solution)/shard_map/ppermute | solution.py:522
  11.8 1.2 %copy-start = (bf16[8,256,256]{2,1,0:T(8,128)(2,1)S(1)}, bf16[8,256,256]{2,1,0:T(8,128)(2,1)}, u32[]{:S(2)}) copy-start(bf16[8,256,256]{2,1,0:T(8,128)(2,1)} %radial.5) | copy-start | bytes 3145732
  11.8 1.2 %copy-start.1 = (bf16[256,256]{1,0:T(8,128)(2,1)S(1)}, bf16[256,256]{1,0:T(8,128)(2,1)}, u32[]{:S(2)}) copy-start(bf16[256,256]{1,0:T(8,128)(2,1)} %feat.1) | copy-start | bytes 393220
  18.9 20.0 %copy-start.2 = (bf16[256,256]{1,0:T(8,128)(2,1)S(1)}, bf16[256,256]{1,0:T(8,128)(2,1)}, u32[]{:S(2)}) copy-start(bf16[256,256]{1,0:T(8,128)(2,1)} %mixing.1) | copy-start | bytes 393220
  40.2 27.2 %all-to-all-start.3 = ((f32[128,1,128]{2,1,0:T(1,128)}), f32[128,1,128]{2,1,0:T(1,128)S(1)}, u32[]{:S(2)}, u32[]{:S(2)}) async-start(f32[128,1,128]{2,1,0:T(1,128)} %bitcast.11), calls=%async_computation.3 | async-start | bytes 131072 | tf_op jit(solution)/shard_map/all_to_all | solution.py:525
  58.2 6.0 %collective-permute-start.1 = (bf16[144,256]{1,0:T(8,128)(2,1)S(1)}, bf16[144,256]{1,0:T(8,128)(2,1)S(1)}, u32[]{:S(2)}, u32[]{:S(2)}) collective-permute-start(bf16[144,256]{1,0:T(8,128)(2,1)S(1)} %get-tuple-element.44), channel_id=1, source_target_pairs={{0,508},{1,5},{2,506},{3,11},{4,0},{5,9},{6,510},{7,15},{8,4},{9,1... | collective-permute-start | bytes 221192 | tf_op jit(solution)/shard_map/ppermute | solution.py:522

commit v5 on v4

--- a/solution.py
+++ b/solution.py
@@ -372,6 +372,13 @@
         weights[u, 0] = high
         weights[u, 1] = (weight - high.astype(F32)).astype(BF16)
 
+    def gather(q):
+        if tile_at is None:
+            home = tile_of(plan[0, q * QUAD])
+            across = [spread[plan[2, q * QUAD + u], home, :] for u in range(QUAD)]
+            kernels = jnp.concatenate([held[u] for u in range(QUAD)], axis=1)
+            grads[...] += dot(kernels, jnp.concatenate(across, axis=0))
+
     def finish(q, u):
         home = plan[0, q * QUAD]
         slot, kind, _, shift, _ = pair_fields(plan, reals, q * QUAD + u)
@@ -381,11 +388,13 @@
         near = monomials(home, -left_shift, -right_shift)
         high, low = weights[u, 0], weights[u, 1]
         sums[slot] += dot(near, jnp.concatenate([high, low], axis=1), NT)
-        grads[tile_at(slot), :] += dot(held[u], spread[kind, tile_of(home), :])
+        if tile_at is not None:
+            grads[tile_at(slot), :] += dot(held[u], spread[kind, tile_of(home), :])
         return dot(far, jnp.concatenate([high, low], axis=0))
 
     def step(q, carry):
         found = begin(q)
+        gather(q - 1)
         parts = []
         for u in range(QUAD):
             parts.append(finish(q - 1, u))
@@ -398,6 +407,7 @@
         for u, found in enumerate(begin(first)):
             hold(u, *found)
         lax.fori_loop(first + 1, last, step, 0)
+        gather(last - 1)
         parts = [finish(last - 1, u) for u in range(QUAD)]
         sums[plan[0, (last - 1) * QUAD]] += sum(parts[1:], parts[0])
 
@@ -419,7 +429,7 @@
     backward_groups(
         plan, reals, 0, plan[3, 0], flipped, places, terms, spread, bases,
         lambda kind, slot: mapped[kind],
-        lambda slot: slice(0, TILE),
+        None,
         grads, sums, held, weights,
     )
     back[0:TILE, :] = grads[...].astype(BF16)

time: 82 us -> 79.7 us (0.972)
  blocking collectives: 32.7 us -> 29.9 us
  waiting for transfers between devices: 5.67 us -> 4.29 us
  starting transfers between devices: 23.5 us -> 24.6 us
    all_to_all x2, blocking collectives: 32.7 us -> 29.9 us  [swap(): return lax.all_to_all(array, axis, 0, 0, tiled=True)]
    ppermute x2, waiting for transfers between devices: 2.66 us -> 0.33 us  [hop(): return lax.ppermute(array, ('dom', 'rep'), ways)]
    all_to_all x2, waiting for transfers between devices: 3.01 us -> 3.96 us  [swap(): return lax.all_to_all(array, axis, 0, 0, tiled=True)]
    all_to_all x2, starting transfers between devices: 17.5 us -> 18.4 us  [swap(): return lax.all_to_all(array, axis, 0, 0, tiled=True)]
  transfers between devices with their start and end apart: 4 -> 4, of which waited for: 3 -> 2; matrix products, arithmetic and copies ran while one was open for 0% -> 0% of each run, Pallas kernels for 14% -> 16%
where the time goes in v5:
time: 79.7 us; the launch traced here: 78.6 us
  blocking collectives  29.9 us (38%)
  starting transfers between devices  24.6 us (31%)
  Pallas kernels  19 us (24%)
  waiting for transfers between devices  4.29 us (5%)
  between operations  0.8 us (1%)
    all_to_all x2, blocking collectives, swap(): return lax.all_to_all(array, axis, 0, 0, tiled=True)  29.9 us
    pallas_call x10, Pallas kernels, call(): pl.pallas_call(kernel, out_shape=[jax.ShapeDtypeStruct(shape, dtype) for...  19 us
    all_to_all x2, starting transfers between devices, swap(): return lax.all_to_all(array, axis, 0, 0, tiled=True)  18.4 us
    ppermute x2, starting transfers between devices, hop(): return lax.ppermute(array, ('dom', 'rep'), ways)  6.23 us
    all_to_all x2, waiting for transfers between devices, swap(): return lax.all_to_all(array, axis, 0, 0, tiled=True)  3.96 us
  transfers between devices with their start and end apart: 4, of which 2 were waited for; matrix products, arithmetic and copies ran while one was open for 0% of the time, Pallas kernels for 16%

profile of v5, /device:TPU:1, one launch (start us, length us, event | category | flops | bytes accessed | tf_op | source)
XLA Modules:
  0.0 78.6 jit_solution(10318941972632517526)
XLA Ops:
  0.6 1.9 %shard_map.139 = (bf16[144,256]{1,0:T(8,128)(2,1)}, s32[32,256]{1,0:T(8,128)}) custom-call(s32[4,128]{1,0:T(4,128)} %hbm_rows.3, s32[1,48]{1,0:T(1,128)} %bitcast.22, s32[1,48]{1,0:T(1,128)} %bitcast.23, s32[1,48]{1,0:T(1,128)} %bitcast.24, s32[3,48]{1,0:T(4,128)} %hbm_image.1, f32[3,256]{1,0:T(4,128)} %hbm_pos.1, bf16[256,256]{1,0:T(8,128)(2,1)} %feat.1), custom_call_target="tpu_custom_call" | custom-call | flops 1073741824 | bytes 1048576 | tf_op jit(solution)/shard_map/pallas_call | solution.py:502
  2.6 0.0 copy-start.3
  2.6 5.1 %all-to-all-start = ((s32[4,8,256]{2,1,0:T(8,128)}), s32[4,8,256]{2,1,0:T(8,128)S(1)}, u32[]{:S(2)}, u32[]{:S(2)}) async-start(s32[4,8,256]{2,1,0:T(8,128)} %bitcast.21), calls=%async_computation | async-start | bytes 65536 | tf_op jit(solution)/shard_map/all_to_all | solution.py:535
  7.7 0.0 copy-start.4
  7.7 0.0 copy-start.5
  7.7 0.0 copy-start.6
  7.7 4.1 %collective-permute-start = (bf16[144,256]{1,0:T(8,128)(2,1)}, bf16[144,256]{1,0:T(8,128)(2,1)S(1)}, u32[]{:S(2)}, u32[]{:S(2)}) collective-permute-start(bf16[144,256]{1,0:T(8,128)(2,1)} %get-tuple-element.33), channel_id=1, source_target_pairs={{0,4},{1,509},{2,10},{3,507},{4,8},{5,1},{6,14},{7,511},{8,12},{9,... | collective-permute-start | bytes 221192 | tf_op jit(solution)/shard_map/ppermute | solution.py:532
  11.8 0.0 copy-done.3
  11.8 0.0 copy-done.4
  11.8 0.0 copy-done.5
  11.8 0.0 copy-done.6
  11.8 0.0 copy-start
  11.8 0.0 copy-start.1
  11.8 0.7 shard_map.138
  12.5 0.0 all-to-all-done
  12.5 0.5 shard_map.140
  13.0 0.0 copy-done
  13.0 0.0 copy-done.1
  13.0 2.4 %shard_map.141 = (bf16[8,256,256]{2,1,0:T(8,128)(2,1)S(1)}, f32[2,128,256]{2,1,0:T(8,128)S(1)}) custom-call(s32[8,256]{1,0:T(8,128)S(1)} %get-tuple-element.31.hbm_plan, f32[8,256]{1,0:T(8,128)S(1)} %get-tuple-element.32.hbm_reals, f32[2,8,128]{2,1,0:T(8,128)S(1)} %get-tuple-element.34.home_places, bf16[2,128,64]{2,1,0:T(8,128)(2,1)S(1)} %get-tuple-element.35.home_terms, ...), custom_call_target="tpu_custom_call" | custom-call | flops 4294967296 | bytes 1048576 | tf_op jit(solution)/shard_map/pallas_call | solution.py:502
  15.4 0.3 collective-permute-done.halo
  15.8 2.8 %shard_map.142 = (bf16[8,128,256]{2,1,0:T(8,128)(2,1)S(1)}, f32[3,8,128]{2,1,0:T(8,128)S(1)}, bf16[3,128,64]{2,1,0:T(8,128)(2,1)S(1)}, bf16[1024,256]{1,0:T(8,128)(2,1)S(1)}) custom-call(s32[8,256]{1,0:T(8,128)S(1)} %get-tuple-element.31.hbm_plan, f32[8,256]{1,0:T(8,128)S(1)} %get-tuple-element.32.hbm_reals, bf16[144,256]{1,0:T(8,128)(2,1)S(1)} %collective-permute-done.halo, ...), custom_call_target="tpu_custom_call" | custom-call | flops 2147483648 | bytes 1048576 | tf_op jit(solution)/shard_map/pallas_call | solution.py:502
  18.5 0.0 copy-start.2
  18.6 19.3 %all_to_all.44 = bf16[4,256,256]{2,1,0:T(8,128)(2,1)S(1)} all-to-all(bf16[4,256,256]{2,1,0:T(8,128)(2,1)S(1)} %bitcast.16), channel_id=1, replica_groups=mesh['dom'=128,'rep'=4] {'rep'}, dimensions={0} | all-to-all | bytes 1048576 | tf_op jit(solution)/shard_map/all_to_all | solution.py:535
  37.8 0.0 copy-done.2
  37.8 1.3 %shard_map.143 = (bf16[256,256]{1,0:T(8,128)(2,1)S(1)}, bf16[2,256,128]{2,1,0:T(8,128)(2,1)S(1)}, f32[128,128]{1,0:T(8,128)}) custom-call(bf16[1024,256]{1,0:T(8,128)(2,1)S(1)} %bitcast.17, bf16[256,256]{1,0:T(8,128)(2,1)S(1)} %copy-done.2, f32[1,256]{1,0:T(1,128)S(1)} %get-tuple-element.38.readout), custom_call_target="tpu_custom_call" | custom-call | flops 268435456 | bytes 1048576 | tf_op jit(solution)/shard_map/pallas_call | solution.py:502
  39.1 13.3 %all-to-all-start.3 = ((f32[128,1,128]{2,1,0:T(1,128)}), f32[128,1,128]{2,1,0:T(1,128)S(1)}, u32[]{:S(2)}, u32[]{:S(2)}) async-start(f32[128,1,128]{2,1,0:T(1,128)} %bitcast.11), calls=%async_computation.3 | async-start | bytes 131072 | tf_op jit(solution)/shard_map/all_to_all | solution.py:535
  52.4 4.6 %shard_map.144 = (bf16[144,256]{1,0:T(8,128)(2,1)S(1)}, bf16[8,256,256]{2,1,0:T(8,128)(2,1)S(1)}, f32[3,32,128]{2,1,0:T(8,128)S(1)}, f32[2,32,128]{2,1,0:T(8,128)S(1)}) custom-call(s32[8,256]{1,0:T(8,128)S(1)} %get-tuple-element.31.hbm_plan, f32[8,256]{1,0:T(8,128)S(1)} %get-tuple-element.32.hbm_reals, bf16[256,256]{1,0:T(8,128)(2,1)S(1)} %get-tuple-element.39.adjoint, ...), custom_call_target="tpu_custom_call" | custom-call | flops 8589934592 | bytes 1048576 | tf_op jit(solution)/shard_map/pallas_call | solution.py:502
  57.1 2.1 %collective-permute-start.1 = (bf16[144,256]{1,0:T(8,128)(2,1)S(1)}, bf16[144,256]{1,0:T(8,128)(2,1)S(1)}, u32[]{:S(2)}, u32[]{:S(2)}) collective-permute-start(bf16[144,256]{1,0:T(8,128)(2,1)S(1)} %get-tuple-element.44), channel_id=1, source_target_pairs={{0,508},{1,5},{2,506},{3,11},{4,0},{5,9},{6,510},{7,15},{8,4},{9,1... | collective-permute-start | bytes 221192 | tf_op jit(solution)/shard_map/ppermute | solution.py:532
  59.2 3.9 %shard_map.145 = (f32[256,256]{1,0:T(8,128)S(1)}, f32[16,256]{1,0:T(8,128)S(1)}) custom-call(s32[8,256]{1,0:T(8,128)S(1)} %get-tuple-element.31.hbm_plan, f32[8,256]{1,0:T(8,128)S(1)} %get-tuple-element.32.hbm_reals, bf16[2,256,128]{2,1,0:T(8,128)(2,1)S(1)} %get-tuple-element.40.flipped, f32[3,8,128]{2,1,0:T(8,128)S(1)} %get-tuple-element.41.places, ...), custom_call_target="tpu_custom_call" | custom-call | flops 4294967296 | bytes 1048576 | tf_op jit(solution)/shard_map/pallas_call | solution.py:502
  63.1 0.0 collective-permute-done.1.got
  63.1 0.2 shard_map.146
  63.3 4.0 %all-to-all-done.3 = f32[128,1,128]{2,1,0:T(1,128)S(1)} async-done(((f32[128,1,128]{2,1,0:T(1,128)}), f32[128,1,128]{2,1,0:T(1,128)S(1)}, u32[]{:S(2)}, u32[]{:S(2)}) %all-to-all-start.3) | async-done | bytes 65568 | tf_op jit(solution)/shard_map/all_to_all | solution.py:535
  67.3 10.6 %all_to_all.45 = bf16[4,288,256]{2,1,0:T(8,128)(2,1)S(1)} all-to-all(bf16[4,288,256]{2,1,0:T(8,128)(2,1)S(1)} %bitcast.14), channel_id=1, replica_groups=mesh['dom'=128,'rep'=4] {'rep'}, dimensions={0} | all-to-all | bytes 1179648 | tf_op jit(solution)/shard_map/all_to_all | solution.py:535
  77.9 0.8 shard_map.147
Async XLA Ops:
  2.6 9.2 %copy-start.3 = (f32[3,256]{1,0:T(4,128)S(1)}, f32[3,256]{1,0:T(4,128)}, u32[]{:S(2)}) copy-start(f32[3,256]{1,0:T(4,128)} %hbm_pos.1) | copy-start | bytes 9220
  2.6 10.0 %all-to-all-start = ((s32[4,8,256]{2,1,0:T(8,128)}), s32[4,8,256]{2,1,0:T(8,128)S(1)}, u32[]{:S(2)}, u32[]{:S(2)}) async-start(s32[4,8,256]{2,1,0:T(8,128)} %bitcast.21), calls=%async_computation | async-start | bytes 65536 | tf_op jit(solution)/shard_map/all_to_all | solution.py:535
  7.7 4.1 %copy-start.4 = (s32[4,128]{1,0:T(4,128)S(1)}, s32[4,128]{1,0:T(4,128)}, u32[]{:S(2)}) copy-start(s32[4,128]{1,0:T(4,128)} %hbm_rows.3) | copy-start | bytes 6148
  7.7 4.1 %copy-start.5 = (f32[256]{0:T(256)S(1)}, f32[256]{0:T(256)}, u32[]{:S(2)}) copy-start(f32[256]{0:T(256)} %param.15) | copy-start | bytes 3076
  7.7 4.1 %copy-start.6 = (f32[8]{0:T(128)S(1)}, f32[8]{0:T(128)}, u32[]{:S(2)}) copy-start(f32[8]{0:T(128)} %hbm_decay.1) | copy-start | bytes 100
  7.7 8.1 %collective-permute-start = (bf16[144,256]{1,0:T(8,128)(2,1)}, bf16[144,256]{1,0:T(8,128)(2,1)S(1)}, u32[]{:S(2)}, u32[]{:S(2)}) collective-permute-start(bf16[144,256]{1,0:T(8,128)(2,1)} %get-tuple-element.33), channel_id=1, source_target_pairs={{0,4},{1,509},{2,10},{3,507},{4,8},{5,1},{6,14},{7,511},{8,12},{9,... | collective-permute-start | bytes 221192 | tf_op jit(solution)/shard_map/ppermute | solution.py:532
  11.8 1.2 %copy-start = (bf16[8,256,256]{2,1,0:T(8,128)(2,1)S(1)}, bf16[8,256,256]{2,1,0:T(8,128)(2,1)}, u32[]{:S(2)}) copy-start(bf16[8,256,256]{2,1,0:T(8,128)(2,1)} %radial.5) | copy-start | bytes 3145732
  11.8 1.2 %copy-start.1 = (bf16[256,256]{1,0:T(8,128)(2,1)S(1)}, bf16[256,256]{1,0:T(8,128)(2,1)}, u32[]{:S(2)}) copy-start(bf16[256,256]{1,0:T(8,128)(2,1)} %feat.1) | copy-start | bytes 393220
  18.5 19.3 %copy-start.2 = (bf16[256,256]{1,0:T(8,128)(2,1)S(1)}, bf16[256,256]{1,0:T(8,128)(2,1)}, u32[]{:S(2)}) copy-start(bf16[256,256]{1,0:T(8,128)(2,1)} %mixing.1) | copy-start | bytes 393220
  39.1 28.1 %all-to-all-start.3 = ((f32[128,1,128]{2,1,0:T(1,128)}), f32[128,1,128]{2,1,0:T(1,128)S(1)}, u32[]{:S(2)}, u32[]{:S(2)}) async-start(f32[128,1,128]{2,1,0:T(1,128)} %bitcast.11), calls=%async_computation.3 | async-start | bytes 131072 | tf_op jit(solution)/shard_map/all_to_all | solution.py:535
  57.1 6.0 %collective-permute-start.1 = (bf16[144,256]{1,0:T(8,128)(2,1)S(1)}, bf16[144,256]{1,0:T(8,128)(2,1)S(1)}, u32[]{:S(2)}, u32[]{:S(2)}) collective-permute-start(bf16[144,256]{1,0:T(8,128)(2,1)S(1)} %get-tuple-element.44), channel_id=1, source_target_pairs={{0,508},{1,5},{2,506},{3,11},{4,0},{5,9},{6,510},{7,15},{8,4},{9,1... | collective-permute-start | bytes 221192 | tf_op jit(solution)/shard_map/ppermute | solution.py:532
